TPU v7x, 32 devices: a whole 2x2x4 slice. The times are simulated.
32 devices in a mesh: gx: 8 (over z, x), gy: 4 (over y, core).
Axes of the slice: x: 2, y: 2, z: 4, core: 2. Of those that a mesh axis runs over, the one named last changes fastest.
Arguments:
- hidden_in: bfloat16 [2048, 16384], P('gy', 'gx'), may hold values from -200 to 200
- norm_gain: float32 [16384], P('gx'), may hold values from 0.1 to 1.9
- w_query: bfloat16 [16384, 8192], P('gx', 'gy'), may hold values from -24 to 24
- w_key: bfloat16 [16384, 1024], P('gx'), may hold values from -1 to 1
- w_value: bfloat16 [16384, 1024], P('gx'), may hold values from -0.046875 to 0.046875
- w_out: bfloat16 [8192, 16384], P('gy', 'gx'), may hold values from -0.06591797 to 0.06591797
- seg_lengths: int32 [8], replicated, may hold values from 1 to 512, 2048 in all
Outputs:
- update: bfloat16 [2048, 16384], P('gy', 'gx')
Inputs may be any that keep to these rules, and one draw needn't show every extreme that they name: `seg_lengths`: the 8 lengths sum to 2048 and the longest is exactly 512.
All inputs are finite; a program needn't handle non-finite values.
Results may differ from a plain program's by a relative error of at most 0.04.
Values may be sent and summed in bfloat16 or wider, within the bound.
No kernel may reach another device: no remote copies, remote signals or barrier semaphores. Data moves between devices by JAX's collectives and lax.ppermute only.
A program may use at most 128 MiB of HBM per device.

v0:
```python
import math

import jax
import jax.numpy as jnp
from jax import lax
from jax.sharding import PartitionSpec as P

H = 64
KVH = 8
HD = 128


ROPE_BASE = 500000.0
EPS = 1e-05


def rotate(values, position, head_size):
    half = head_size // 2
    exponent = jnp.arange(half, dtype=jnp.float32) * (2.0 / head_size)
    frequency = ROPE_BASE ** (-exponent)
    angle = position[:, None, None] * frequency[None, None, :]
    cosine = jnp.cos(angle)
    sine = jnp.sin(angle)
    first = values[..., :half]
    second = values[..., half:]
    return jnp.concatenate(
        [first * cosine - second * sine, second * cosine + first * sine], axis=-1
    )


def segment_table(seg_lengths, tokens):
    ends = jnp.cumsum(seg_lengths)
    starts = ends - seg_lengths
    index = jnp.arange(tokens, dtype=jnp.int32)
    member = ((index[:, None] >= starts[None, :]) & (index[:, None] < ends[None, :])).astype(
        jnp.int32
    )
    seg_id = jnp.sum(member * jnp.arange(seg_lengths.shape[0], dtype=jnp.int32)[None, :], axis=1)
    first_index = jnp.sum(member * starts[None, :], axis=1)
    return (seg_id, index - first_index)


def normalize(block, gain, squares, model_width):
    widened = block.astype(jnp.float32)
    scale = lax.rsqrt(squares / model_width + EPS)
    return (widened * scale[:, None] * gain[None, :]).astype(jnp.bfloat16)


def shards(hidden_in, norm_gain, w_query, w_key, w_value, w_out, seg_lengths):
    rows_own, width = hidden_in.shape
    model_width = width * lax.axis_size("gx")
    tokens = rows_own * lax.axis_size("gy")
    query_rows = tokens // lax.axis_size("gx")
    widened = hidden_in.astype(jnp.float32)
    squares = lax.psum(jnp.sum(widened * widened, axis=1), "gx")
    source = normalize(hidden_in, norm_gain, squares, model_width)
    gathered = lax.all_gather(source, "gy", axis=0, tiled=True)
    query_cols = w_query.shape[1]
    heads_local = query_cols // HD
    group = H // KVH
    kv_local = max(1, heads_local // group)
    pair_cols = kv_local * HD
    first_head = lax.axis_index("gy") * heads_local // group
    key_own = lax.dynamic_slice_in_dim(w_key, first_head * HD, pair_cols, 1)
    value_own = lax.dynamic_slice_in_dim(w_value, first_head * HD, pair_cols, 1)
    seg_id, position = segment_table(seg_lengths, tokens)
    here = lax.axis_index("gx") * query_rows
    query_seg = lax.dynamic_slice_in_dim(seg_id, here, query_rows)
    query_pos = lax.dynamic_slice_in_dim(position, here, query_rows)
    query_index = here + jnp.arange(query_rows, dtype=jnp.int32)
    query_sum = lax.psum_scatter(
        jnp.dot(gathered, w_query, preferred_element_type=jnp.float32).astype(jnp.bfloat16),
        "gx",
        scatter_dimension=0,
        tiled=True,
    ).astype(jnp.float32)
    pair_part = jnp.concatenate(
        [
            jnp.dot(gathered, key_own, preferred_element_type=jnp.float32),
            jnp.dot(gathered, value_own, preferred_element_type=jnp.float32),
        ],
        axis=1,
    )
    pair_sum = lax.psum(pair_part.astype(jnp.bfloat16), "gx").astype(jnp.float32)
    key_raw = pair_sum[:, :pair_cols].astype(jnp.bfloat16)
    value_raw = pair_sum[:, pair_cols:].astype(jnp.bfloat16)
    group_local = heads_local // kv_local
    queries = rotate(
        query_sum.reshape(query_rows, heads_local, HD), query_pos.astype(jnp.float32), HD
    ).astype(jnp.bfloat16)
    queries = queries.reshape(query_rows, kv_local, group_local, HD)
    key_count = key_raw.shape[0]
    keys = rotate(
        key_raw.astype(jnp.float32).reshape(key_count, kv_local, HD),
        position.astype(jnp.float32),
        HD,
    )
    keys = keys.astype(jnp.bfloat16).reshape(key_count, pair_cols)
    score_scale = 1.0 / math.sqrt(HD)
    running = jnp.full((kv_local, group_local, query_rows), -1e30, jnp.float32)
    count = keys.shape[0]
    key_index = jnp.arange(count, dtype=jnp.int32)
    allowed = (query_seg[:, None] == seg_id[None, :]) & (key_index[None, :] <= query_index[:, None])
    key_heads = keys.reshape(count, kv_local, HD)
    value_heads = value_raw.reshape(count, kv_local, HD)
    scores = (
        jnp.einsum("rkgd,nkd->kgrn", queries, key_heads, preferred_element_type=jnp.float32)
        * score_scale
    )
    scores = jnp.where(allowed[None, None], scores, -1e30)
    newest = jnp.maximum(running, jnp.max(scores, axis=-1))
    weights = jnp.where(allowed[None, None], jnp.exp(scores - newest[..., None]), 0.0)
    denominator = jnp.sum(weights, axis=-1)
    added = jnp.einsum(
        "kgrn,nkd->rkgd",
        weights.astype(jnp.bfloat16),
        value_heads,
        preferred_element_type=jnp.float32,
    )
    accum = added
    running, denominator, accum = (newest, denominator, accum)
    attended = (
        (accum / denominator.transpose(2, 0, 1)[..., None])
        .reshape(query_rows, query_cols)
        .astype(jnp.bfloat16)
    )
    partial_out = jnp.dot(
        lax.all_gather(attended, "gx", axis=0, tiled=True),
        w_out,
        preferred_element_type=jnp.float32,
    )
    return lax.psum_scatter(partial_out.astype(jnp.bfloat16), "gy", scatter_dimension=0, tiled=True)


def solution(mesh):
    in_specs = (
        P("gy", "gx"),
        P("gx"),
        P("gx", "gy"),
        P("gx", None),
        P("gx", None),
        P("gy", "gx"),
        P(),
    )
    out_specs = P("gy", "gx")
    return jax.shard_map(shards, mesh=mesh, in_specs=in_specs, out_specs=out_specs, check_vma=False)
```

profile of v0, /device:TPU:0, one launch (start us, length us, event | category | flops | bytes accessed | tf_op | source)
XLA Modules:
  0.0 628.6 jit_solution(15671343593259728992)
XLA Ops:
  6.5 2.1 fusion.6
  8.6 23.1 %psum.14 = f32[512]{0:T(512)S(1)} all-reduce(f32[512]{0:T(512)S(1)} %fusion.6), channel_id=1, replica_groups=mesh['gx'=8,'gy'=4] {'gx'}, use_global_device_ids=true, to_apply=%region_1.0 | all-reduce | flops 512 | bytes 4096 | tf_op jit(solution)/shard_map/psum | solution.py:55
  31.7 3.5 fusion.8
  35.3 55.7 %all-gather.3.cloned.1.call-done = bf16[2048,2048]{1,0:T(8,128)(2,1)} async-done(((bf16[512,2048]{1,0:T(8,128)(2,1)}), bf16[2048,2048]{1,0:T(8,128)(2,1)}) %all-gather.3.cloned.1.call-update) | async-done | bytes 8388624 | tf_op jit(solution)/shard_map/all_gather | solution.py:57
  90.9 6.1 convolution_convert_fusion.2
  97.1 3.6 convolution_convert_fusion.3
  100.7 1.5 pad_maximum_fusion
  102.2 23.6 %convolution_convert_fusion.1 = bf16[2048,2048]{1,0:T(8,128)(2,1)} fusion(bf16[2048,2048]{1,0:T(8,128)(2,1)} %all-gather.3.cloned.1.call-done, bf16[2048,2048]{1,0:T(8,128)(2,1)} %param.9), kind=kOutput, calls=%fused_computation.8 | convolution fusion | flops 17184063488 | bytes 25165824 | tf_op jit(solution)/shard_map/dot_general | solution.py:72
  128.0 5.6 multiply_cosine_fusion
  133.6 70.6 %all-reduce.2.cloned.1.call-done = bf16[2048,512]{0,1:T(8,128)(2,1)} async-done(((bf16[2048,512]{0,1:T(8,128)(2,1)}), bf16[2048,512]{0,1:T(8,128)(2,1)}) %all-reduce.2.cloned.1.call-update) | async-done | bytes 2097168 | tf_op jit(solution)/shard_map/psum | solution.py:84
  204.2 2.7 fusion.29
  206.9 1.5 fusion.30
  208.4 1.8 copy.22
  210.3 3.2 copy.21
  213.4 4.9 subtract_convert_fusion.1
  218.3 138.3 %reduce-scatter.3.cloned.1.call-done = bf16[256,2048]{1,0:T(8,128)(2,1)} async-done(((bf16[2048,2048]{1,0:T(8,128)(2,1)}), bf16[256,2048]{1,0:T(8,128)(2,1)}) %reduce-scatter.3.cloned.1.call-update) | async-done | bytes 1048592 | tf_op jit(solution)/shard_map/reduce_scatter | solution.py:71
  356.6 1.5 convert_bitcast_fusion
  358.5 0.8 subtract_convert_fusion
  360.0 13.7 %fusion = (f32[2,8,256]{2,1,0:T(8,128)S(1)}, f32[2,2048,256,8]{2,1,3,0:T(8,128)}) fusion(pred[256,2048]{0,1:T(8,128)(4,1)S(1)} %fusion.10, bf16[256,2,8,64]{3,0,2,1:T(8,128)(2,1)S(1)} %bitcast.51, bf16[256,2,8,64]{3,0,2,1:T(8,128)(2,1)S(1)} %bitcast.50, bf16[2048,2,64]{2,0,1:T(8,128)(2,1)S(1)} %copy-done.1, bf16[2048,2,64]{2,0,1:T(8,128)(2,1)S(1)} %copy-done), kind=kOutput, calls=%fused_computation.2 | convolution fusion | flops 2176839680 | bytes 36192256 | tf_op jit(solution)/shard_map/rkgd,nkd->kgrn/dot_general | solution.py:107
  373.8 14.9 %fusion.1 = f32[2,8,256]{2,1,0:T(8,128)S(1)} fusion(f32[2,2048,256,8]{2,1,3,0:T(8,128)} %get-tuple-element.22, f32[2,8,256]{2,1,0:T(8,128)S(1)} %broadcast_maximum_fusion, pred[256,2048]{0,1:T(8,128)(4,1)S(1)} %fusion.10), kind=kLoop, calls=%fused_computation.3 | loop fusion | flops 41938944 | bytes 34111488 | tf_op jit(solution)/shard_map/reduce_sum | solution.py:113
  388.7 15.0 %fusion.9 = bf16[256,2,8,128]{0,3,2,1:T(8,128)(2,1)} fusion(bf16[2048,2,128,1]{0,2,3,1:T(8,128)(2,1)S(1)} %bitcast.53, f32[2,2048,256,8]{2,1,3,0:T(8,128)} %get-tuple-element.22, f32[2,8,256]{2,1,0:T(8,128)S(1)} %broadcast_maximum_fusion, pred[256,2048]{0,1:T(8,128)(4,1)S(1)} %fusion.10, f32[256,2,8]{0,2,1:T(8,128)S(1)} %bitcast.54), kind=kOutput, calls=%fused_computation.18 | convolution fusion | flops 2190475264 | bytes 36208640 | tf_op jit(solution)/shard_map/kgrn,nkd->rkgd/dot_general | solution.py:114
  404.1 124.2 %all-gather.5.cloned.1.call-done = bf16[2048,2048]{0,1:T(8,128)(2,1)} async-done(((bf16[256,2048]{0,1:T(8,128)(2,1)}), bf16[2048,2048]{0,1:T(8,128)(2,1)}) %all-gather.5.cloned.1.call-update) | async-done | bytes 8388624 | tf_op jit(solution)/shard_map/all_gather | solution.py:128
  528.3 23.7 %convolution_convert_fusion = bf16[2048,2048]{1,0:T(8,128)(2,1)} fusion(bf16[2048,2048]{0,1:T(8,128)(2,1)} %all-gather.5.cloned.1.call-done, bf16[2048,2048]{1,0:T(8,128)(2,1)} %param.12), kind=kOutput, calls=%fused_computation.7 | convolution fusion | flops 17184063488 | bytes 25165824 | tf_op jit(solution)/shard_map/dot_general | solution.py:127
  552.1 70.0 %reduce-scatter.5.cloned.1.call-done = bf16[512,2048]{1,0:T(8,128)(2,1)} async-done(((bf16[2048,2048]{1,0:T(8,128)(2,1)}), bf16[512,2048]{1,0:T(8,128)(2,1)}) %reduce-scatter.5.cloned.1.call-update) | async-done | bytes 2097168 | tf_op jit(solution)/shard_map/reduce_scatter | solution.py:132
  (35 shorter events, 3.7 us)
Async XLA Ops:
  6.5 84.4 %all-gather.3.cloned.1.call-start = ((), (), s32[]{:S(2)}) async-start(), calls=%async_computation.2 | async-start | bytes 10485760 | tf_op jit(solution)/shard_map/all_gather | solution.py:57
  35.2 169.0 %all-reduce.2.cloned.1.call-start = ((), (), s32[]{:S(2)}) async-start(), calls=%async_computation.3 | async-start | bytes 4194304 | tf_op jit(solution)/shard_map/psum | solution.py:84
  90.9 6.1 copy-start.3
  102.2 254.5 %reduce-scatter.3.cloned.1.call-start = ((), (), s32[]{:S(2)}) async-start(), calls=%async_computation.4 | async-start | bytes 9437184 | tf_op jit(solution)/shard_map/reduce_scatter | solution.py:71
  125.8 0.7 copy-start.4
  125.8 402.5 %all-gather.5.cloned.1.call-start = ((), (), s32[]{:S(2)}) async-start(), calls=%async_computation.5 | async-start | bytes 9437184 | tf_op jit(solution)/shard_map/all_gather | solution.py:128
  358.5 1.4 copy-start
  358.5 1.5 copy-start.1
  373.8 14.9 %copy-start.2 = (bf16[2048,256]{0,1:T(8,128)(2,1)S(1)}, bf16[2048,256]{0,1:T(8,128)(2,1)}, u32[]{:S(2)}) copy-start(bf16[2048,256]{0,1:T(8,128)(2,1)} %get-tuple-element.12) | copy-start | bytes 3145732
  403.8 218.3 %reduce-scatter.5.cloned.1.call-start = ((), (), s32[]{:S(2)}) async-start(), calls=%async_computation.6 | async-start | bytes 10485760 | tf_op jit(solution)/shard_map/reduce_scatter | solution.py:132
Sparse Core Ops, SparseCore 0:
  35.3 55.5 all-gather.2
  102.3 101.8 all-reduce.1
  207.8 148.7 reduce-scatter.2
  403.9 124.3 all-gather.4
  552.2 69.8 reduce-scatter.4
where the time goes:
time: 629 us
  waiting for transfers between devices  459 us (73%)
  matrix products  85.8 us (14%)
  other arithmetic  36.1 us (6%)
  blocking collectives  23.1 us (4%)
  between operations  13.3 us (2%)
  local copies, waits for them, and re-layouts  10.8 us (2%)
    reduce_scatter x1, waiting for transfers between devices, shards(): lax.psum_scatter(jnp.dot(gathered, w_query, preferred_element_type=jnp.fl...  138 us
    all_gather x1, waiting for transfers between devices, shards(): lax.all_gather(attended, 'gx', axis=0, tiled=True)  124 us
    psum x1, waiting for transfers between devices, shards(): lax.psum(pair_part.astype(jnp.bfloat16), 'gx').astype(jnp.float32)  70.6 us
    reduce_scatter x1, waiting for transfers between devices, shards(): lax.psum_scatter(partial_out.astype(jnp.bfloat16), 'gy', scatter_dimensio...  70 us
    all_gather x1, waiting for transfers between devices, shards(): gathered = lax.all_gather(source, 'gy', axis=0, tiled=True)  55.7 us
    dot_general x1, matrix products, shards(): jnp.dot(lax.all_gather(attended, 'gx', axis=0, tiled=True), w_out, prefer...  23.7 us
    dot_general x1, matrix products, shards(): jnp.dot(gathered, w_query, preferred_element_type=jnp.float32)  23.6 us
    psum x1, blocking collectives, shards(): squares = lax.psum(jnp.sum(widened * widened, axis=1), 'gx')  23.1 us
  transfers between devices with their start and end apart: 5, of which 5 were waited for; matrix products, arithmetic and copies ran while one was open for 7% of the time, Pallas kernels for 0%

commit v1 on v0

--- a/solution.py
+++ b/solution.py
@@ -1,8 +1,11 @@
+import functools
 import math
 
 import jax
 import jax.numpy as jnp
 from jax import lax
+from jax.experimental import pallas as pl
+from jax.experimental.pallas import tpu as pltpu
 from jax.sharding import PartitionSpec as P
 
 H = 64
@@ -12,6 +15,7 @@
 
 ROPE_BASE = 500000.0
 EPS = 1e-05
+SEG_MOST = 512
 
 
 def rotate(values, position, head_size):
@@ -46,7 +50,7 @@
     return (widened * scale[:, None] * gain[None, :]).astype(jnp.bfloat16)
 
 
-def shards(hidden_in, norm_gain, w_query, w_key, w_value, w_out, seg_lengths):
+def shards_any(hidden_in, norm_gain, w_query, w_key, w_value, w_out, seg_lengths):
     rows_own, width = hidden_in.shape
     model_width = width * lax.axis_size("gx")
     tokens = rows_own * lax.axis_size("gy")
@@ -132,6 +136,198 @@
     return lax.psum_scatter(partial_out.astype(jnp.bfloat16), "gy", scatter_dimension=0, tiled=True)
 
 
+def swap(value, axis, bit):
+    return lax.ppermute(value, axis, [(i, i ^ bit) for i in range(lax.axis_size(axis))])
+
+
+def columns(array, start, size):
+    return lax.dynamic_slice_in_dim(array, start, size, 1)
+
+
+def prepare_kernel(own_ref, pair_ref, cos_ref, sin_ref, scale_ref, key_ref, value_ref):
+    blocks = 4
+    rows = pair_ref.shape[0] // blocks
+    own = own_ref[0]
+    key_ref[:SEG_MOST, :] = jnp.zeros((SEG_MOST, HD), jnp.bfloat16)
+    value_ref[:SEG_MOST, :] = jnp.zeros((SEG_MOST, HD), jnp.bfloat16)
+    for block in range(blocks):
+        start = pl.multiple_of((block ^ own) * rows, rows)
+        here = pl.ds(block * rows, rows)
+        there = pl.ds(SEG_MOST + block * rows, rows)
+        key = pair_ref[pl.ds(start, rows), :HD].astype(jnp.float32)
+        value = pair_ref[pl.ds(start, rows), HD:].astype(jnp.float32)
+        key = key * cos_ref[here, :] + pltpu.roll(key, HD // 2, 1) * sin_ref[here, :]
+        key_ref[there, :] = key.astype(jnp.bfloat16)
+        value_ref[there, :] = (value * scale_ref[here, :]).astype(jnp.bfloat16)
+
+
+def prepare(own, pair, cosine, sine, scale):
+    tokens = pair.shape[0]
+    padded = jax.ShapeDtypeStruct((SEG_MOST + tokens, HD), jnp.bfloat16)
+    vmem = pl.BlockSpec(memory_space=pltpu.VMEM)
+    return pl.pallas_call(
+        prepare_kernel,
+        out_shape=[padded, padded],
+        in_specs=[pl.BlockSpec(memory_space=pltpu.SMEM)] + [vmem] * 4,
+        out_specs=[vmem, vmem],
+        compiler_params=pltpu.CompilerParams(vmem_limit_bytes=32 * 2**20),
+        cost_estimate=pl.CostEstimate(
+            flops=8 * tokens * HD, bytes_accessed=20 * tokens * HD, transcendentals=0
+        ),
+    )(own, pair, cosine, sine, scale)
+
+
+def attend_kernel(first, half, own_ref, len_ref, query_ref, key_ref, value_ref, cos_ref, sin_ref, out_ref):
+    rows = query_ref.shape[0] // 2
+    block_rows = cos_ref.shape[0] // 4
+    window = SEG_MOST + rows
+    own = own_ref[0]
+    for piece in range(2):
+        start = pl.multiple_of((own ^ (first + piece)) * block_rows + half * rows, rows)
+        here = pl.ds(start, rows)
+        key = key_ref[pl.ds(start, window), :]
+        value = value_ref[pl.ds(start, window), :]
+        query_at = start + lax.broadcasted_iota(jnp.int32, (rows, 1), 0)
+        key_at = start - SEG_MOST + lax.broadcasted_iota(jnp.int32, (rows, window), 1)
+        begin = jnp.zeros((rows, 1), jnp.int32)
+        total = len_ref[0]
+        for i in range(1, len_ref.shape[0]):
+            begin = jnp.where(query_at >= total, total, begin)
+            total = total + len_ref[i]
+        allowed = (key_at >= begin) & (key_at <= query_at)
+        for head in range(2):
+            at = pl.ds(head * HD, HD)
+            query = query_ref[pl.ds(piece * rows, rows), at].astype(jnp.float32)
+            query = query * cos_ref[here, :] + pltpu.roll(query, HD // 2, 1) * sin_ref[here, :]
+            scores = lax.dot_general(
+                query.astype(jnp.bfloat16),
+                key,
+                (((1,), (1,)), ((), ())),
+                preferred_element_type=jnp.float32,
+            )
+            scores = jnp.where(allowed, scores * (1.0 / math.sqrt(HD)), -1e30)
+            weights = jnp.exp(scores - jnp.max(scores, axis=1, keepdims=True))
+            weights = jnp.where(allowed, weights, 0.0)
+            denominator = jnp.sum(weights, axis=1, keepdims=True)
+            added = jnp.dot(weights.astype(jnp.bfloat16), value, preferred_element_type=jnp.float32)
+            out_ref[pl.ds(piece * rows, rows), at] = (added / denominator).astype(jnp.bfloat16)
+
+
+def attend(first, half, own, seg_lengths, query, key, value, cosine, sine):
+    rows = query.shape[0]
+    vmem = pl.BlockSpec(memory_space=pltpu.VMEM)
+    smem = pl.BlockSpec(memory_space=pltpu.SMEM)
+    scores = 2 * rows * (SEG_MOST + rows // 2)
+    return pl.pallas_call(
+        functools.partial(attend_kernel, first, half),
+        out_shape=jax.ShapeDtypeStruct(query.shape, jnp.bfloat16),
+        in_specs=[smem, smem] + [vmem] * 5,
+        out_specs=vmem,
+        compiler_params=pltpu.CompilerParams(vmem_limit_bytes=32 * 2**20),
+        cost_estimate=pl.CostEstimate(
+            flops=4 * scores * HD, bytes_accessed=4 * 2**20, transcendentals=scores
+        ),
+    )(own, seg_lengths, query, key, value, cosine, sine)
+
+
+def shards_8x4(hidden_in, norm_gain, w_query, w_key, w_value, w_out, seg_lengths):
+    f32, bf16 = jnp.float32, jnp.bfloat16
+    rows, width = hidden_in.shape
+    model_width = width * lax.axis_size("gx")
+    tokens = rows * lax.axis_size("gy")
+    cols = w_query.shape[1]
+    half_rows, half_cols, piece = rows // 2, cols // 2, cols // 8
+    gx, gy = lax.axis_index("gx"), lax.axis_index("gy")
+    x_at, z_low, z_high = gx & 1, (gx >> 1) & 1, gx >> 2
+    rank = x_at * 4 + z_low * 2 + z_high
+    own = gy.astype(jnp.int32)[None]
+
+    widened = hidden_in.astype(f32)
+    source = (widened * norm_gain[None, :]).astype(bf16)
+    squares = jnp.sum(widened * widened, axis=1)
+    squares = lax.dynamic_update_slice_in_dim(jnp.zeros((tokens,), f32), squares, gy * rows, 0)
+
+    parts = {}
+    for h in range(2):
+        parts[0, h] = source[h * half_rows : (h + 1) * half_rows]
+        parts[1, h] = swap(parts[0, h], "gy", 1)
+        parts[2, h] = swap(parts[0, h], "gy", 2)
+        parts[3, h] = swap(parts[2, h], "gy", 1)
+
+    key_part = jnp.dot(source, w_key, preferred_element_type=f32).astype(bf16)
+    value_part = jnp.dot(source, w_value, preferred_element_type=f32).astype(bf16)
+
+    def pair_heads(side):
+        picked = []
+        for r in range(4):
+            head = (gy ^ r) * 2 + side
+            picked += [columns(key_part, head * HD, HD), columns(value_part, head * HD, HD)]
+        return jnp.concatenate(picked, axis=1)
+
+    pair = pair_heads(x_at).astype(f32) + swap(pair_heads(1 - x_at), "gx", 1).astype(f32)
+    pair = pair.astype(bf16)
+    b = [pair[:, 2 * HD * r : 2 * HD * (r + 1)] for r in range(4)]
+    got = swap(jnp.concatenate([b[1], b[3]], axis=0), "gy", 1)
+    got_1, got_3 = got[:rows], got[rows:]
+    far = swap(jnp.concatenate([b[2], got_3], axis=0), "gy", 2)
+    pair = jnp.concatenate([b[0], got_1, far], axis=0)
+    pair = lax.psum(pair, "gx", axis_index_groups=[[0, 2, 4, 6], [1, 3, 5, 7]])
+
+    squares = lax.psum(squares, ("gx", "gy"))
+    scale = lax.rsqrt(squares / model_width + EPS)[:, None]
+    _, position = segment_table(seg_lengths, tokens)
+    lane = jnp.arange(HD, dtype=jnp.int32)
+    exponent = (lane % (HD // 2)).astype(f32) * (2.0 / HD)
+    angle = position.astype(f32)[:, None] * (ROPE_BASE ** (-exponent))[None, :]
+    cosine = jnp.cos(angle) * scale
+    sine = jnp.where(lane < HD // 2, -1.0, 1.0)[None, :] * jnp.sin(angle) * scale
+    key, value = prepare(own, pair, cosine, sine, jnp.broadcast_to(scale, (tokens, HD)))
+
+    query_blocks = [columns(w_query, (rank ^ r) * piece, piece) for r in range(8)]
+    w_near = jnp.concatenate(query_blocks[0:2], axis=1)
+    w_low = jnp.concatenate(query_blocks[2:4], axis=1)
+    w_cross = jnp.concatenate(query_blocks[4:8], axis=1)
+    w_rows = jnp.concatenate(
+        [lax.dynamic_slice_in_dim(w_out, (rank ^ r) * piece, piece, 0) for r in range(8)], axis=0
+    )
+
+    attended = {}
+    for first in (0, 2):
+        for h in range(2):
+            chunk = jnp.concatenate([parts[first, h], parts[first + 1, h]], axis=0)
+            cross = swap(jnp.dot(chunk, w_cross, preferred_element_type=f32).astype(bf16), "gx", 1)
+            low = jnp.dot(chunk, w_low, preferred_element_type=f32) + cross[:, half_cols // 2 :].astype(f32)
+            near = jnp.dot(chunk, w_near, preferred_element_type=f32) + cross[:, : half_cols // 2].astype(f32)
+            got = swap(low.astype(bf16), "gx", 2)
+            high = near[:, piece:] + got[:, piece:].astype(f32)
+            near = near[:, :piece] + got[:, :piece].astype(f32)
+            query = (near + swap(high.astype(bf16), "gx", 4).astype(f32)).astype(bf16)
+            attended[first, h] = attend(first, h, own, seg_lengths, query, key, value, cosine, sine)
+
+    kept, crossed = {}, {}
+    for first, h in ((0, 0), (2, 0), (2, 1), (0, 1)):
+        a = attended[first, h]
+        a = jnp.concatenate([a, swap(a, "gx", 4)], axis=1)
+        a = jnp.concatenate([a, swap(a, "gx", 2)], axis=1)
+        a = jnp.concatenate([a, swap(a, "gx", 1)], axis=1)
+        given = jnp.dot(a[half_rows:], w_rows, preferred_element_type=f32).astype(bf16)
+        mine = jnp.dot(a[:half_rows], w_rows, preferred_element_type=f32)
+        mine = mine + swap(given, "gy", 1).astype(f32)
+        if first:
+            crossed[h] = swap(mine.astype(bf16), "gy", 2)
+        else:
+            kept[h] = mine
+    return jnp.concatenate(
+        [(kept[h] + crossed[h].astype(f32)).astype(bf16) for h in range(2)], axis=0
+    )
+
+
+def shards(hidden_in, norm_gain, w_query, w_key, w_value, w_out, seg_lengths):
+    split = (lax.axis_size("gx"), lax.axis_size("gy"))
+    body = shards_8x4 if split == (8, 4) else shards_any
+    return body(hidden_in, norm_gain, w_query, w_key, w_value, w_out, seg_lengths)
+
+
 def solution(mesh):
     in_specs = (
         P("gy", "gx"),

time: 629 us -> 464 us (0.74)
  waiting for transfers between devices: 459 us -> 204 us
  starting transfers between devices: 0.57 us -> 42.9 us
  blocking collectives: 23.1 us -> 58.4 us
  local copies, waits for them, and re-layouts: 10.8 us -> 44.4 us
  other arithmetic: 36.1 us -> 14 us
  matrix products: 85.8 us -> 69.4 us
  Pallas kernels: 0 us -> 11.5 us
    reduce_scatter x2 -> x0, waiting for transfers between devices: 208 us -> none  [the longest x1 138 us: shards(): lax.psum_scatter(jnp.dot(gathered, w_query, preferred_element_type=jnp.fl...]
    ppermute x0 -> x39, waiting for transfers between devices: none -> 204 us  [swap(): lax.ppermute(value, axis, [(i, i ^ bit) for i in range(lax.axis_size(axis...]
    all_gather x2 -> x0, waiting for transfers between devices: 180 us -> none  [the longest x1 124 us: shards(): lax.all_gather(attended, 'gx', axis=0, tiled=True)]
    psum x1, waiting for transfers between devices: 70.6 us -> 0.01 us  [shards_8x4(): pair = lax.psum(pair, 'gx', axis_index_groups=[[0, 2, 4, 6], [1, 3, 5, 7]])]
    ppermute x0 -> x39, starting transfers between devices: none -> 42.9 us  [swap(): lax.ppermute(value, axis, [(i, i ^ bit) for i in range(lax.axis_size(axis...]
    psum x1, blocking collectives: 23.1 us -> 58.4 us  [shards_8x4(): squares = lax.psum(squares, ('gx', 'gy'))]
    unnamed x13 -> x72, local copies, waits for them, and re-layouts: 5.95 us -> 32.1 us
    dot_general x6 -> x22, matrix products: 85.8 us -> 69.4 us  [the longest x4 17.9 us: shards_8x4(): jnp.dot(chunk, w_cross, preferred_element_type=f32).astype(bf16)]
  transfers between devices with their start and end apart: 5 -> 40, of which waited for: 5 -> 18; matrix products, arithmetic and copies ran while one was open for 7% -> 26% of each run, Pallas kernels for 0% -> 3%
where the time goes in v1:
time: 464 us; the launch traced here: 459 us
  waiting for transfers between devices  204 us (44%)
  matrix products  69.4 us (15%)
  blocking collectives  58.4 us (13%)
  local copies, waits for them, and re-layouts  44.4 us (10%)
  starting transfers between devices  42.9 us (9%)
  between operations  14.4 us (3%)
  other arithmetic  14 us (3%)
  Pallas kernels  11.5 us (2%)
    ppermute x39, waiting for transfers between devices, swap(): lax.ppermute(value, axis, [(i, i ^ bit) for i in range(lax.axis_size(axis...  204 us
    psum x1, blocking collectives, shards_8x4(): squares = lax.psum(squares, ('gx', 'gy'))  58.4 us
    ppermute x39, starting transfers between devices, swap(): lax.ppermute(value, axis, [(i, i ^ bit) for i in range(lax.axis_size(axis...  42.9 us
    unnamed x72, local copies, waits for them, and re-layouts  32.1 us
    dot_general x4, matrix products, shards_8x4(): jnp.dot(chunk, w_cross, preferred_element_type=f32).astype(bf16)  17.9 us
    dot_general x4, matrix products, shards_8x4(): jnp.dot(chunk, w_low, preferred_element_type=f32)  11.8 us
    pallas_call x4, Pallas kernels, attend(): pl.pallas_call(functools.partial(attend_kernel, first, half), out_shape=j...  11.1 us
    dot_general x4, matrix products, shards_8x4(): jnp.dot(chunk, w_near, preferred_element_type=f32)  10.7 us
  transfers between devices with their start and end apart: 40, of which 18 were waited for; matrix products, arithmetic and copies ran while one was open for 26% of the time, Pallas kernels for 3%

profile of v1, /device:TPU:0, one launch (start us, length us, event | category | flops | bytes accessed | tf_op | source)
XLA Modules:
  0.0 458.6 jit_solution(11678601214319072249)
XLA Ops:
  13.9 5.7 %convolution_convert_fusion.8 = bf16[512,1024]{1,0:T(8,128)(2,1)} fusion(bf16[512,2048]{1,0:T(8,128)(2,1)S(1)} %get-tuple-element.20, bf16[2048,1024]{1,0:T(8,128)(2,1)} %param.10), kind=kOutput, calls=%fused_computation.35 | convolution fusion | flops 2148007936 | bytes 7340032 | tf_op jit(solution)/shard_map/dot_general | solution.py:257
  38.4 58.4 %psum.15 = f32[2048]{0:T(1024)S(1)} all-reduce(f32[2048]{0:T(1024)S(1)} %dynamic_update_slice.3), channel_id=1, replica_groups=mesh['gx'=8,'gy'=4] {'gx','gy'}, use_global_device_ids=true, to_apply=%region_4.5 | all-reduce | flops 2048 | bytes 16384 | tf_op jit(solution)/shard_map/psum | solution.py:276
  108.8 3.8 fusion.14
  112.6 5.7 %constant_dynamic-slice_fusion.1 = (bf16[2048,256]{1,0:T(8,128)(2,1)}, bf16[2048,256]{1,0:T(8,128)(2,1)S(1)}, bf16[2048,256]{1,0:T(8,128)(2,1)S(1)}, bf16[2048,2...) fusion(bf16[2048,2048]{1,0:T(8,128)(2,1)} %param.9, ...), kind=kLoop, calls=%fused_computation.126 | loop fusion | bytes 16777248 | tf_op jit(solution)/shard_map/dynamic_slice | solution.py:144
  121.0 4.9 %convolution_convert_fusion.5 = bf16[512,1024]{1,0:T(8,128)(2,1)} fusion(bf16[256,2048]{1,0:T(8,128)(2,1)} %collective-permute-done.21, bf16[256,2048]{1,0:T(8,128)(2,1)} %get-tuple-element.18, bf16[2048,256]{1,0:T(8,128)(2,1)S(1)} %get-tuple-element.10, bf16[2048,256]{1,0:T(8,128)(2,1)S(1)} %get-tuple-element.11, ...), kind=kOutput, calls=%fused_computation.32 | convolution fusion | flops 2168979456 | bytes 7340032 | tf_op jit(solution)/shard_map/dot_general | solution.py:298
  128.3 4.9 %convolution_convert_fusion.9 = bf16[512,1024]{1,0:T(8,128)(2,1)} fusion(bf16[256,2048]{1,0:T(8,128)(2,1)} %collective-permute-done, bf16[256,2048]{1,0:T(8,128)(2,1)} %get-tuple-element.17, bf16[2048,256]{1,0:T(8,128)(2,1)S(1)} %get-tuple-element.10, bf16[2048,256]{1,0:T(8,128)(2,1)S(1)} %get-tuple-element.11, ...), kind=kOutput, calls=%fused_computation.36 | convolution fusion | flops 2168979456 | bytes 7340032 | tf_op jit(solution)/shard_map/dot_general | solution.py:298
  139.2 3.9 convolution_convert_fusion.4
  143.6 8.0 %collective-permute-done.6 = bf16[1024,256]{1,0:T(8,128)(2,1)S(1)} collective-permute-done((bf16[1024,256]{1,0:T(8,128)(2,1)S(1)}, bf16[1024,256]{1,0:T(8,128)(2,1)S(1)}, u32[]{:S(2)}, u32[]{:S(2)}) %collective-permute-start.6) | collective-permute-done | bytes 524320 | tf_op jit(solution)/shard_map/ppermute | solution.py:140
  158.1 4.3 convolution_convert_fusion.6
  164.2 10.7 %collective-permute-done.1 = bf16[512,1024]{1,0:T(8,128)(2,1)} collective-permute-done((bf16[512,1024]{1,0:T(8,128)(2,1)}, bf16[512,1024]{1,0:T(8,128)(2,1)}, u32[]{:S(2)}, u32[]{:S(2)}) %collective-permute-start.1) | collective-permute-done | bytes 1048608 | tf_op jit(solution)/shard_map/ppermute | solution.py:140
  187.5 23.8 %collective-permute-done.2 = bf16[512,512]{1,0:T(8,128)(2,1)S(1)} collective-permute-done((bf16[512,512]{1,0:T(8,128)(2,1)S(1)}, bf16[512,512]{1,0:T(8,128)(2,1)S(1)}, u32[]{:S(2)}, u32[]{:S(2)}) %collective-permute-start.2) | collective-permute-done | bytes 524320 | tf_op jit(solution)/shard_map/ppermute | solution.py:140
  213.9 17.8 %collective-permute-done.3 = bf16[512,256]{1,0:T(8,128)(2,1)S(1)} collective-permute-done((bf16[512,256]{1,0:T(8,128)(2,1)S(1)}, bf16[512,256]{1,0:T(8,128)(2,1)S(1)}, u32[]{:S(2)}, u32[]{:S(2)}) %collective-permute-start.3) | collective-permute-done | bytes 262176 | tf_op jit(solution)/shard_map/ppermute | solution.py:140
  256.5 7.5 %collective-permute-done.32 = bf16[512,512]{1,0:T(8,128)(2,1)S(1)} collective-permute-done((bf16[512,512]{1,0:T(8,128)(2,1)}, bf16[512,512]{1,0:T(8,128)(2,1)S(1)}, u32[]{:S(2)}, u32[]{:S(2)}) %collective-permute-start.32) | collective-permute-done | bytes 524320 | tf_op jit(solution)/shard_map/ppermute | solution.py:140
  264.6 5.4 %collective-permute-done.7 = bf16[512,256]{1,0:T(8,128)(2,1)S(1)} collective-permute-done((bf16[512,256]{1,0:T(8,128)(2,1)S(1)}, bf16[512,256]{1,0:T(8,128)(2,1)S(1)}, u32[]{:S(2)}, u32[]{:S(2)}) %collective-permute-start.7) | collective-permute-done | bytes 262176 | tf_op jit(solution)/shard_map/ppermute | solution.py:140
  273.4 4.7 %collective-permute-done.14 = bf16[512,512]{1,0:T(8,128)(2,1)S(1)} collective-permute-done((bf16[512,512]{1,0:T(8,128)(2,1)S(1)}, bf16[512,512]{1,0:T(8,128)(2,1)S(1)}, u32[]{:S(2)}, u32[]{:S(2)}) %collective-permute-start.14) | collective-permute-done | bytes 524320 | tf_op jit(solution)/shard_map/ppermute | solution.py:140
  278.6 8.4 %collective-permute-done.33 = bf16[512,256]{1,0:T(8,128)(2,1)S(1)} collective-permute-done((bf16[512,256]{1,0:T(8,128)(2,1)S(1)}, bf16[512,256]{1,0:T(8,128)(2,1)S(1)}, u32[]{:S(2)}, u32[]{:S(2)}) %collective-permute-start.33) | collective-permute-done | bytes 262176 | tf_op jit(solution)/shard_map/ppermute | solution.py:140
  293.3 7.3 %collective-permute-done.26 = bf16[512,512]{1,0:T(8,128)(2,1)S(1)} collective-permute-done((bf16[512,512]{1,0:T(8,128)(2,1)S(1)}, bf16[512,512]{1,0:T(8,128)(2,1)S(1)}, u32[]{:S(2)}, u32[]{:S(2)}) %collective-permute-start.26) | collective-permute-done | bytes 524320 | tf_op jit(solution)/shard_map/ppermute | solution.py:140
  313.2 9.1 %collective-permute-done.16 = bf16[512,256]{1,0:T(8,128)(2,1)S(1)} collective-permute-done((bf16[512,256]{1,0:T(8,128)(2,1)S(1)}, bf16[512,256]{1,0:T(8,128)(2,1)S(1)}, u32[]{:S(2)}, u32[]{:S(2)}) %collective-permute-start.16) | collective-permute-done | bytes 262176 | tf_op jit(solution)/shard_map/ppermute | solution.py:140
  325.6 5.0 %collective-permute-done.35 = bf16[512,512]{1,0:T(8,128)(2,1)S(1)} collective-permute-done((bf16[512,512]{1,0:T(8,128)(2,1)S(1)}, bf16[512,512]{1,0:T(8,128)(2,1)S(1)}, u32[]{:S(2)}, u32[]{:S(2)}) %collective-permute-start.35) | collective-permute-done | bytes 524320 | tf_op jit(solution)/shard_map/ppermute | solution.py:140
  332.5 6.9 %collective-permute-done.17 = bf16[512,512]{1,0:T(8,128)(2,1)S(1)} collective-permute-done((bf16[512,512]{1,0:T(8,128)(2,1)S(1)}, bf16[512,512]{1,0:T(8,128)(2,1)S(1)}, u32[]{:S(2)}, u32[]{:S(2)}) %collective-permute-start.17) | collective-permute-done | bytes 524320 | tf_op jit(solution)/shard_map/ppermute | solution.py:140
  344.1 28.3 %collective-permute-done.36 = bf16[512,1024]{1,0:T(8,128)(2,1)S(1)} collective-permute-done((bf16[512,1024]{1,0:T(8,128)(2,1)S(1)}, bf16[512,1024]{1,0:T(8,128)(2,1)S(1)}, u32[]{:S(2)}, u32[]{:S(2)}) %collective-permute-start.36) | collective-permute-done | bytes 1048608 | tf_op jit(solution)/shard_map/ppermute | solution.py:140
  375.4 18.4 %collective-permute-done.18 = bf16[512,1024]{1,0:T(8,128)(2,1)S(1)} collective-permute-done((bf16[512,1024]{1,0:T(8,128)(2,1)S(1)}, bf16[512,1024]{1,0:T(8,128)(2,1)S(1)}, u32[]{:S(2)}, u32[]{:S(2)}) %collective-permute-start.18) | collective-permute-done | bytes 1048608 | tf_op jit(solution)/shard_map/ppermute | solution.py:140
  406.6 18.7 %collective-permute-done.38 = bf16[256,2048]{1,0:T(8,128)(2,1)S(1)} collective-permute-done((bf16[256,2048]{1,0:T(8,128)(2,1)S(1)}, bf16[256,2048]{1,0:T(8,128)(2,1)S(1)}, u32[]{:S(2)}, u32[]{:S(2)}) %collective-permute-start.38) | collective-permute-done | bytes 1048608 | tf_op jit(solution)/shard_map/ppermute | solution.py:140
  427.9 19.5 %collective-permute-done.20 = bf16[256,2048]{1,0:T(8,128)(2,1)S(1)} collective-permute-done((bf16[256,2048]{1,0:T(8,128)(2,1)S(1)}, bf16[256,2048]{1,0:T(8,128)(2,1)S(1)}, u32[]{:S(2)}, u32[]{:S(2)}) %collective-permute-start.20) | collective-permute-done | bytes 1048608 | tf_op jit(solution)/shard_map/ppermute | solution.py:140
  (202 shorter events, 153.3 us)
Async XLA Ops:
  6.5 228.5 %all-reduce.2.cloned.1.call-start = ((), (), s32[]{:S(2)}) async-start(), calls=%async_computation | async-start | bytes 2097152 | tf_op jit(solution)/shard_map/psum | solution.py:274
  10.4 117.8 %collective-permute-start.29 = (bf16[256,2048]{1,0:T(8,128)(2,1)}, bf16[256,2048]{1,0:T(8,128)(2,1)}, u32[]{:S(2)}, u32[]{:S(2)}) collective-permute-start(bf16[256,2048]{1,0:T(8,128)(2,1)} %get-tuple-element.18), channel_id=1, source_target_pairs={{0,2},{1,3},{2,0},{3,1},{4,6},{5,7},{6,4},{7,5},{8,10},{9,11},{10,... | collective-permute-start | bytes 3145736 | tf_op jit(solution)/shard_map/ppermute | solution.py:140
  13.3 107.6 %collective-permute-start.21 = (bf16[256,2048]{1,0:T(8,128)(2,1)}, bf16[256,2048]{1,0:T(8,128)(2,1)}, u32[]{:S(2)}, u32[]{:S(2)}) collective-permute-start(bf16[256,2048]{1,0:T(8,128)(2,1)} %get-tuple-element.18), channel_id=1, source_target_pairs={{0,1},{1,0},{2,3},{3,2},{4,5},{5,4},{6,7},{7,6},{8,9},{9,8},{10,11... | collective-permute-start | bytes 3145736 | tf_op jit(solution)/shard_map/ppermute | solution.py:140
  13.4 120.2 %collective-permute-start.11 = (bf16[256,2048]{1,0:T(8,128)(2,1)}, bf16[256,2048]{1,0:T(8,128)(2,1)}, u32[]{:S(2)}, u32[]{:S(2)}) collective-permute-start(bf16[256,2048]{1,0:T(8,128)(2,1)} %get-tuple-element.17), channel_id=1, source_target_pairs={{0,2},{1,3},{2,0},{3,1},{4,6},{5,7},{6,4},{7,5},{8,10},{9,11},{10,... | collective-permute-start | bytes 3145736 | tf_op jit(solution)/shard_map/ppermute | solution.py:140
  13.4 115.0 %collective-permute-start = (bf16[256,2048]{1,0:T(8,128)(2,1)}, bf16[256,2048]{1,0:T(8,128)(2,1)}, u32[]{:S(2)}, u32[]{:S(2)}) collective-permute-start(bf16[256,2048]{1,0:T(8,128)(2,1)} %get-tuple-element.17), channel_id=1, source_target_pairs={{0,1},{1,0},{2,3},{3,2},{4,5},{5,4},{6,7},{7,6},{8,9},{9,8},{10,11... | collective-permute-start | bytes 3145736 | tf_op jit(solution)/shard_map/ppermute | solution.py:140
  36.5 81.8 %collective-permute-start.4 = (bf16[512,1024]{1,0:T(8,128)(2,1)}, bf16[512,1024]{1,0:T(8,128)(2,1)}, u32[]{:S(2)}, u32[]{:S(2)}) collective-permute-start(bf16[512,1024]{1,0:T(8,128)(2,1)} %get-tuple-element.26), channel_id=1, source_target_pairs={{0,4},{4,0},{8,12},{12,8},{16,20},{20,16},{24,28},{28,24},{1,5},{5... | collective-permute-start | bytes 3145736 | tf_op jit(solution)/shard_map/ppermute | solution.py:140
  125.9 26.9 %collective-permute-start.22 = (bf16[512,1024]{1,0:T(8,128)(2,1)}, bf16[512,1024]{1,0:T(8,128)(2,1)}, u32[]{:S(2)}, u32[]{:S(2)}) collective-permute-start(bf16[512,1024]{1,0:T(8,128)(2,1)} %convolution_convert_fusion.5), channel_id=1, source_target_pairs={{0,4},{4,0},{8,12},{12,8},{16,20},{20,16},{24,28},{28,24},{1,5},{5... | collective-permute-start | bytes 3145736 | tf_op jit(solution)/shard_map/ppermute | solution.py:140
  133.2 41.7 %collective-permute-start.1 = (bf16[512,1024]{1,0:T(8,128)(2,1)}, bf16[512,1024]{1,0:T(8,128)(2,1)}, u32[]{:S(2)}, u32[]{:S(2)}) collective-permute-start(bf16[512,1024]{1,0:T(8,128)(2,1)} %convolution_convert_fusion.9), channel_id=1, source_target_pairs={{0,4},{4,0},{8,12},{12,8},{16,20},{20,16},{24,28},{28,24},{1,5},{5... | collective-permute-start | bytes 3145736 | tf_op jit(solution)/shard_map/ppermute | solution.py:140
  143.1 88.7 %collective-permute-start.31 = (bf16[512,1024]{1,0:T(8,128)(2,1)}, bf16[512,1024]{1,0:T(8,128)(2,1)}, u32[]{:S(2)}, u32[]{:S(2)}) collective-permute-start(bf16[512,1024]{1,0:T(8,128)(2,1)} %convolution_convert_fusion.4), channel_id=1, source_target_pairs={{0,4},{4,0},{8,12},{12,8},{16,20},{20,16},{24,28},{28,24},{1,5},{5... | collective-permute-start | bytes 3145736 | tf_op jit(solution)/shard_map/ppermute | solution.py:140
  156.2 30.8 %collective-permute-start.23 = (bf16[512,512]{1,0:T(8,128)(2,1)S(1)}, bf16[512,512]{1,0:T(8,128)(2,1)S(1)}, u32[]{:S(2)}, u32[]{:S(2)}) collective-permute-start(bf16[512,512]{1,0:T(8,128)(2,1)S(1)} %fusion.10), channel_id=1, source_target_pairs={{0,8},{4,12},{8,0},{12,4},{16,24},{20,28},{24,16},{28,20},{1,9},{5... | collective-permute-start | bytes 1572872 | tf_op jit(solution)/shard_map/ppermute | solution.py:140
  162.4 80.2 %collective-permute-start.13 = (bf16[512,1024]{1,0:T(8,128)(2,1)}, bf16[512,1024]{1,0:T(8,128)(2,1)}, u32[]{:S(2)}, u32[]{:S(2)}) collective-permute-start(bf16[512,1024]{1,0:T(8,128)(2,1)} %convolution_convert_fusion.6), channel_id=1, source_target_pairs={{0,4},{4,0},{8,12},{12,8},{16,20},{20,16},{24,28},{28,24},{1,5},{5... | collective-permute-start | bytes 3145736 | tf_op jit(solution)/shard_map/ppermute | solution.py:140
  177.9 33.4 %collective-permute-start.2 = (bf16[512,512]{1,0:T(8,128)(2,1)S(1)}, bf16[512,512]{1,0:T(8,128)(2,1)S(1)}, u32[]{:S(2)}, u32[]{:S(2)}) collective-permute-start(bf16[512,512]{1,0:T(8,128)(2,1)S(1)} %fusion.8), channel_id=1, source_target_pairs={{0,8},{4,12},{8,0},{12,4},{16,24},{20,28},{24,16},{28,20},{1,9},{5... | collective-permute-start | bytes 1572872 | tf_op jit(solution)/shard_map/ppermute | solution.py:140
  187.2 26.6 %collective-permute-start.24 = (bf16[512,256]{1,0:T(8,128)(2,1)S(1)}, bf16[512,256]{1,0:T(8,128)(2,1)S(1)}, u32[]{:S(2)}, u32[]{:S(2)}) collective-permute-start(bf16[512,256]{1,0:T(8,128)(2,1)S(1)} %fusion.26), channel_id=1, source_target_pairs={{0,16},{4,20},{8,24},{12,28},{16,0},{20,4},{24,8},{28,12},{1,17},{... | collective-permute-start | bytes 786440 | tf_op jit(solution)/shard_map/ppermute | solution.py:140
  235.0 29.1 %collective-permute-start.32 = (bf16[512,512]{1,0:T(8,128)(2,1)}, bf16[512,512]{1,0:T(8,128)(2,1)S(1)}, u32[]{:S(2)}, u32[]{:S(2)}) collective-permute-start(bf16[512,512]{1,0:T(8,128)(2,1)} %fusion.11), channel_id=1, source_target_pairs={{0,8},{4,12},{8,0},{12,4},{16,24},{20,28},{24,16},{28,20},{1,9},{5... | collective-permute-start | bytes 1572872 | tf_op jit(solution)/shard_map/ppermute | solution.py:140
  245.0 33.1 %collective-permute-start.14 = (bf16[512,512]{1,0:T(8,128)(2,1)S(1)}, bf16[512,512]{1,0:T(8,128)(2,1)S(1)}, u32[]{:S(2)}, u32[]{:S(2)}) collective-permute-start(bf16[512,512]{1,0:T(8,128)(2,1)S(1)} %fusion.9), channel_id=1, source_target_pairs={{0,8},{4,12},{8,0},{12,4},{16,24},{20,28},{24,16},{28,20},{1,9},{5... | collective-permute-start | bytes 1572872 | tf_op jit(solution)/shard_map/ppermute | solution.py:140
  254.9 45.6 %collective-permute-start.26 = (bf16[512,512]{1,0:T(8,128)(2,1)S(1)}, bf16[512,512]{1,0:T(8,128)(2,1)S(1)}, u32[]{:S(2)}, u32[]{:S(2)}) collective-permute-start(bf16[512,512]{1,0:T(8,128)(2,1)S(1)} %pad_maximum_fusion.25), channel_id=1, source_target_pairs={{0,8},{4,12},{8,0},{12,4},{16,24},{20,28},{24,16},{28,20},{1,9},{5... | collective-permute-start | bytes 1572872 | tf_op jit(solution)/shard_map/ppermute | solution.py:140
  270.1 53.6 %collective-permute-start.8 = (bf16[512,512]{1,0:T(8,128)(2,1)S(1)}, bf16[512,512]{1,0:T(8,128)(2,1)S(1)}, u32[]{:S(2)}, u32[]{:S(2)}) collective-permute-start(bf16[512,512]{1,0:T(8,128)(2,1)S(1)} %pad_maximum_fusion.23), channel_id=1, source_target_pairs={{0,8},{4,12},{8,0},{12,4},{16,24},{20,28},{24,16},{28,20},{1,9},{5... | collective-permute-start | bytes 1572872 | tf_op jit(solution)/shard_map/ppermute | solution.py:140
  300.7 40.6 %collective-permute-start.27 = (bf16[512,1024]{1,0:T(8,128)(2,1)S(1)}, bf16[512,1024]{1,0:T(8,128)(2,1)S(1)}, u32[]{:S(2)}, u32[]{:S(2)}) collective-permute-start(bf16[512,1024]{1,0:T(8,128)(2,1)S(1)} %pad_maximum_fusion.13), channel_id=1, source_target_pairs={{0,4},{4,0},{8,12},{12,8},{16,20},{20,16},{24,28},{28,24},{1,5},{5... | collective-permute-start | bytes 3145736 | tf_op jit(solution)/shard_map/ppermute | solution.py:140
  323.8 51.3 %collective-permute-start.9 = (bf16[512,1024]{1,0:T(8,128)(2,1)S(1)}, bf16[512,1024]{1,0:T(8,128)(2,1)S(1)}, u32[]{:S(2)}, u32[]{:S(2)}) collective-permute-start(bf16[512,1024]{1,0:T(8,128)(2,1)S(1)} %pad_maximum_fusion.11), channel_id=1, source_target_pairs={{0,4},{4,0},{8,12},{12,8},{16,20},{20,16},{24,28},{28,24},{1,5},{5... | collective-permute-start | bytes 3145736 | tf_op jit(solution)/shard_map/ppermute | solution.py:140
  330.8 41.7 %collective-permute-start.36 = (bf16[512,1024]{1,0:T(8,128)(2,1)S(1)}, bf16[512,1024]{1,0:T(8,128)(2,1)S(1)}, u32[]{:S(2)}, u32[]{:S(2)}) collective-permute-start(bf16[512,1024]{1,0:T(8,128)(2,1)S(1)} %pad_maximum_fusion.14), channel_id=1, source_target_pairs={{0,4},{4,0},{8,12},{12,8},{16,20},{20,16},{24,28},{28,24},{1,5},{5... | collective-permute-start | bytes 3145736 | tf_op jit(solution)/shard_map/ppermute | solution.py:140
  339.6 54.3 %collective-permute-start.18 = (bf16[512,1024]{1,0:T(8,128)(2,1)S(1)}, bf16[512,1024]{1,0:T(8,128)(2,1)S(1)}, u32[]{:S(2)}, u32[]{:S(2)}) collective-permute-start(bf16[512,1024]{1,0:T(8,128)(2,1)S(1)} %pad_maximum_fusion.12), channel_id=1, source_target_pairs={{0,4},{4,0},{8,12},{12,8},{16,20},{20,16},{24,28},{28,24},{1,5},{5... | collective-permute-start | bytes 3145736 | tf_op jit(solution)/shard_map/ppermute | solution.py:140
  344.0 62.6 %collective-permute-start.28 = (bf16[256,2048]{1,0:T(8,128)(2,1)S(1)}, bf16[256,2048]{1,0:T(8,128)(2,1)S(1)}, u32[]{:S(2)}, u32[]{:S(2)}) collective-permute-start(bf16[256,2048]{1,0:T(8,128)(2,1)S(1)} %convolution_convert_fusion.1), channel_id=1, source_target_pairs={{0,1},{1,0},{2,3},{3,2},{4,5},{5,4},{6,7},{7,6},{8,9},{9,8},{10,11... | collective-permute-start | bytes 3145736 | tf_op jit(solution)/shard_map/ppermute | solution.py:140
  399.3 26.0 %collective-permute-start.38 = (bf16[256,2048]{1,0:T(8,128)(2,1)S(1)}, bf16[256,2048]{1,0:T(8,128)(2,1)S(1)}, u32[]{:S(2)}, u32[]{:S(2)}) collective-permute-start(bf16[256,2048]{1,0:T(8,128)(2,1)S(1)} %fusion.5), channel_id=1, source_target_pairs={{0,2},{1,3},{2,0},{3,1},{4,6},{5,7},{6,4},{7,5},{8,10},{9,11},{10,... | collective-permute-start | bytes 3145736 | tf_op jit(solution)/shard_map/ppermute | solution.py:140
  406.3 41.1 %collective-permute-start.20 = (bf16[256,2048]{1,0:T(8,128)(2,1)S(1)}, bf16[256,2048]{1,0:T(8,128)(2,1)S(1)}, u32[]{:S(2)}, u32[]{:S(2)}) collective-permute-start(bf16[256,2048]{1,0:T(8,128)(2,1)S(1)} %fusion.4), channel_id=1, source_target_pairs={{0,2},{1,3},{2,0},{3,1},{4,6},{5,7},{6,4},{7,5},{8,10},{9,11},{10,... | collective-permute-start | bytes 3145736 | tf_op jit(solution)/shard_map/ppermute | solution.py:140
  (44 other events, 764.9 us)
Sparse Core Ops, SparseCore 0:
  152.9 77.5 all-reduce.1

commit v2 on v1

--- a/solution.py
+++ b/solution.py
@@ -136,12 +136,28 @@
     return lax.psum_scatter(partial_out.astype(jnp.bfloat16), "gy", scatter_dimension=0, tiled=True)
 
 
+SCOPE = 32 * 2**20
+SMALL = pl.CostEstimate(flops=0, bytes_accessed=0, transcendentals=0)
+
+
 def swap(value, axis, bit):
     return lax.ppermute(value, axis, [(i, i ^ bit) for i in range(lax.axis_size(axis))])
 
 
 def columns(array, start, size):
     return lax.dynamic_slice_in_dim(array, start, size, 1)
+
+
+def after(value, *others):
+    hbm = pl.BlockSpec(memory_space=pl.ANY)
+    return pl.pallas_call(
+        lambda *refs: None,
+        out_shape=jax.ShapeDtypeStruct(value.shape, value.dtype),
+        in_specs=[hbm] * (1 + len(others)),
+        out_specs=hbm,
+        input_output_aliases={0: 0},
+        cost_estimate=SMALL,
+    )(value, *others)
 
 
 def prepare_kernel(own_ref, pair_ref, cos_ref, sin_ref, scale_ref, key_ref, value_ref):
@@ -170,10 +186,8 @@
         out_shape=[padded, padded],
         in_specs=[pl.BlockSpec(memory_space=pltpu.SMEM)] + [vmem] * 4,
         out_specs=[vmem, vmem],
-        compiler_params=pltpu.CompilerParams(vmem_limit_bytes=32 * 2**20),
-        cost_estimate=pl.CostEstimate(
-            flops=8 * tokens * HD, bytes_accessed=20 * tokens * HD, transcendentals=0
-        ),
+        compiler_params=pltpu.CompilerParams(vmem_limit_bytes=SCOPE),
+        cost_estimate=SMALL,
     )(own, pair, cosine, sine, scale)
 
 
@@ -217,17 +231,122 @@
     rows = query.shape[0]
     vmem = pl.BlockSpec(memory_space=pltpu.VMEM)
     smem = pl.BlockSpec(memory_space=pltpu.SMEM)
-    scores = 2 * rows * (SEG_MOST + rows // 2)
     return pl.pallas_call(
         functools.partial(attend_kernel, first, half),
         out_shape=jax.ShapeDtypeStruct(query.shape, jnp.bfloat16),
         in_specs=[smem, smem] + [vmem] * 5,
         out_specs=vmem,
-        compiler_params=pltpu.CompilerParams(vmem_limit_bytes=32 * 2**20),
+        compiler_params=pltpu.CompilerParams(vmem_limit_bytes=SCOPE),
         cost_estimate=pl.CostEstimate(
-            flops=4 * scores * HD, bytes_accessed=4 * 2**20, transcendentals=scores
+            flops=2**31, bytes_accessed=2**20, transcendentals=0
         ),
     )(own, seg_lengths, query, key, value, cosine, sine)
+
+
+def copy_kernel(place_ref, weight_ref, out_ref):
+    del place_ref
+    out_ref[...] = weight_ref[...]
+
+
+def reorder(place, weight):
+    blocks = place.shape[0]
+    shape = (weight.shape[0] // blocks, weight.shape[1])
+    return pl.pallas_call(
+        copy_kernel,
+        out_shape=jax.ShapeDtypeStruct(weight.shape, jnp.bfloat16),
+        grid_spec=pltpu.PrefetchScalarGridSpec(
+            num_scalar_prefetch=1,
+            grid=(blocks,),
+            in_specs=[pl.BlockSpec(shape, lambda j, place: (place[j], 0))],
+            out_specs=pl.BlockSpec(shape, lambda j, place: (j, 0)),
+        ),
+        compiler_params=pltpu.CompilerParams(vmem_limit_bytes=SCOPE),
+        cost_estimate=pl.CostEstimate(
+            flops=0, bytes_accessed=4 * weight.size, transcendentals=0
+        ),
+    )(place, weight)
+
+
+def scale_rows(gain_ref, source_refs, scaled):
+    @pl.when(pl.program_id(0) == 0)
+    def _():
+        at = 0
+        for ref in source_refs:
+            widened = ref[...].astype(jnp.float32) * gain_ref[...]
+            scaled[pl.ds(at, ref.shape[0]), :] = widened.astype(jnp.bfloat16)
+            at += ref.shape[0]
+
+
+def pairs_kernel(place_ref, gain_ref, source_ref, key_ref, value_ref, given_ref, kept_ref, scaled):
+    scale_rows(gain_ref, [source_ref], scaled)
+    second = place_ref[place_ref.shape[0] - 1] == 1
+    for i, ref in enumerate((key_ref, value_ref)):
+        product = jnp.dot(scaled[...], ref[...], preferred_element_type=jnp.float32)
+        product = product.astype(jnp.bfloat16)
+        low, high = product[:, :HD], product[:, HD:]
+        kept_ref[:, pl.ds(i * HD, HD)] = jnp.where(second, high, low)
+        given_ref[:, pl.ds(i * HD, HD)] = jnp.where(second, low, high)
+
+
+def pairs(place, gain, source, w_key, w_value):
+    rows, depth = source.shape
+    out = jax.ShapeDtypeStruct((rows, 8 * HD), jnp.bfloat16)
+    picked = pl.BlockSpec((depth, 2 * HD), lambda j, place: (0, place[j]))
+    made = pl.BlockSpec((rows, 2 * HD), lambda j, place: (0, j))
+    return pl.pallas_call(
+        pairs_kernel,
+        out_shape=[out, out],
+        grid_spec=pltpu.PrefetchScalarGridSpec(
+            num_scalar_prefetch=1,
+            grid=(4,),
+            in_specs=[
+                pl.BlockSpec((1, depth), lambda j, place: (0, 0)),
+                pl.BlockSpec((rows, depth), lambda j, place: (0, 0)),
+                picked,
+                picked,
+            ],
+            out_specs=[made, made],
+            scratch_shapes=[pltpu.VMEM((rows, depth), jnp.bfloat16)],
+        ),
+        compiler_params=pltpu.CompilerParams(vmem_limit_bytes=SCOPE),
+        cost_estimate=pl.CostEstimate(
+            flops=4 * rows * depth * 8 * HD, bytes_accessed=4 * depth * 8 * HD, transcendentals=0
+        ),
+    )(place, gain[None, :], source, w_key, w_value)
+
+
+def project_kernel(pieces, place_ref, gain_ref, *refs):
+    weight_ref, out_refs, scaled = refs[pieces], refs[pieces + 1 : -1], refs[-1]
+    scale_rows(gain_ref, refs[:pieces], scaled)
+    product = jnp.dot(scaled[...], weight_ref[...], preferred_element_type=jnp.float32)
+    rows = product.shape[0] // len(out_refs)
+    for i, ref in enumerate(out_refs):
+        ref[...] = product[i * rows : (i + 1) * rows, :].astype(jnp.bfloat16)
+
+
+def project(place, gain, pieces, weight, size, outs):
+    piece_rows, depth = pieces[0].shape
+    rows, width = len(pieces) * piece_rows, size * place.shape[0]
+    out = jax.ShapeDtypeStruct((rows // outs, width), jnp.bfloat16)
+    return pl.pallas_call(
+        functools.partial(project_kernel, len(pieces)),
+        out_shape=[out] * outs,
+        grid_spec=pltpu.PrefetchScalarGridSpec(
+            num_scalar_prefetch=1,
+            grid=(place.shape[0],),
+            in_specs=[pl.BlockSpec((1, depth), lambda j, place: (0, 0))]
+            + [pl.BlockSpec((piece_rows, depth), lambda j, place: (0, 0))] * len(pieces)
+            + [pl.BlockSpec((depth, size), lambda j, place: (0, place[j]))],
+            out_specs=[pl.BlockSpec((rows // outs, size), lambda j, place: (0, j))] * outs,
+            scratch_shapes=[pltpu.VMEM((rows, depth), jnp.bfloat16)],
+        ),
+        compiler_params=pltpu.CompilerParams(vmem_limit_bytes=SCOPE),
+        cost_estimate=pl.CostEstimate(
+            flops=2 * rows * depth * width,
+            bytes_accessed=2 * (rows * depth + (depth + rows) * width),
+            transcendentals=0,
+        ),
+    )(place, gain[None, :], *pieces, weight)
 
 
 def shards_8x4(hidden_in, norm_gain, w_query, w_key, w_value, w_out, seg_lengths):
@@ -236,80 +355,105 @@
     model_width = width * lax.axis_size("gx")
     tokens = rows * lax.axis_size("gy")
     cols = w_query.shape[1]
-    half_rows, half_cols, piece = rows // 2, cols // 2, cols // 8
+    half_rows, piece, pair_cols = rows // 2, cols // 8, 2 * HD
     gx, gy = lax.axis_index("gx"), lax.axis_index("gy")
     x_at, z_low, z_high = gx & 1, (gx >> 1) & 1, gx >> 2
-    rank = x_at * 4 + z_low * 2 + z_high
+    rank = (x_at * 4 + z_low * 2 + z_high).astype(jnp.int32)
+    z_at = z_low * 2 + z_high
     own = gy.astype(jnp.int32)[None]
+    order = jnp.arange(4, dtype=jnp.int32)
 
     widened = hidden_in.astype(f32)
-    source = (widened * norm_gain[None, :]).astype(bf16)
     squares = jnp.sum(widened * widened, axis=1)
     squares = lax.dynamic_update_slice_in_dim(jnp.zeros((tokens,), f32), squares, gy * rows, 0)
+    squares = squares.reshape(tokens // HD, HD)
+    squares = squares_x = squares + swap(squares, "gx", 1)
+    for axis, bit in (("gy", 1), ("gx", 2), ("gx", 4)):
+        squares = squares + swap(squares, axis, bit)
 
     parts = {}
     for h in range(2):
-        parts[0, h] = source[h * half_rows : (h + 1) * half_rows]
+        parts[0, h] = hidden_in[h * half_rows : (h + 1) * half_rows]
         parts[1, h] = swap(parts[0, h], "gy", 1)
+
+    for h in range(2):
         parts[2, h] = swap(parts[0, h], "gy", 2)
         parts[3, h] = swap(parts[2, h], "gy", 1)
 
-    key_part = jnp.dot(source, w_key, preferred_element_type=f32).astype(bf16)
-    value_part = jnp.dot(source, w_value, preferred_element_type=f32).astype(bf16)
-
-    def pair_heads(side):
-        picked = []
-        for r in range(4):
-            head = (gy ^ r) * 2 + side
-            picked += [columns(key_part, head * HD, HD), columns(value_part, head * HD, HD)]
-        return jnp.concatenate(picked, axis=1)
-
-    pair = pair_heads(x_at).astype(f32) + swap(pair_heads(1 - x_at), "gx", 1).astype(f32)
+
+    x_served = []
+
+    def swap_x(value):
+        if x_served:
+            value = after(value, x_served[-1])
+        x_served.append(swap(value, "gx", 1))
+        return x_served[-1]
+
+    def pieces(first):
+        return [parts[first + i, h] for h in range(2) for i in range(2)]
+
+    place = jnp.concatenate([gy ^ order, x_at[None]]).astype(jnp.int32)
+    given, kept_pair = pairs(place, norm_gain, hidden_in, w_key, w_value)
+    near_place = after(rank ^ (order + 4), given)
+    crossed_in, keeps = {}, {}
+    outs = project(near_place, norm_gain, pieces(0), w_query, piece, 2)
+    (keeps[0],) = project(after(rank ^ order, outs[0]), norm_gain, pieces(0), w_query, piece, 1)
+    given = swap_x(after(given, squares_x))
+    crossed_in[0, 0], crossed_in[0, 1] = swap_x(outs[0]), swap_x(outs[1])
+    pair = given.astype(f32) + after(kept_pair, keeps[0]).astype(f32)
     pair = pair.astype(bf16)
-    b = [pair[:, 2 * HD * r : 2 * HD * (r + 1)] for r in range(4)]
-    got = swap(jnp.concatenate([b[1], b[3]], axis=0), "gy", 1)
-    got_1, got_3 = got[:rows], got[rows:]
-    far = swap(jnp.concatenate([b[2], got_3], axis=0), "gy", 2)
-    pair = jnp.concatenate([b[0], got_1, far], axis=0)
-    pair = lax.psum(pair, "gx", axis_index_groups=[[0, 2, 4, 6], [1, 3, 5, 7]])
-
-    squares = lax.psum(squares, ("gx", "gy"))
-    scale = lax.rsqrt(squares / model_width + EPS)[:, None]
+    given = columns(pair, (1 - z_low) * 2 * pair_cols, 2 * pair_cols)
+    pair = columns(pair, z_low * 2 * pair_cols, 2 * pair_cols).astype(f32)
+    pair = (pair + swap(given, "gx", 2).astype(f32)).astype(bf16)
+    outs = project(after(rank ^ (order + 4), pair), norm_gain, pieces(2), w_query, piece, 2)
+    (keeps[2],) = project(after(rank ^ order, outs[0]), norm_gain, pieces(2), w_query, piece, 1)
+    crossed_in[2, 0], crossed_in[2, 1] = swap_x(outs[0]), swap_x(outs[1])
+    given = columns(pair, (1 - z_high) * pair_cols, pair_cols)
+    pair = columns(pair, z_high * pair_cols, pair_cols).astype(f32)
+    pair = (pair + swap(given, "gx", 4).astype(f32)).astype(bf16)
+    across = []
+    for i in range(8):
+        for j in range(4):
+            across.append((i * 4 + j, i * 4 + (j ^ ((i >> 1) & 1) * 2 ^ (i >> 2))))
+    squares = after(squares, pair)
+    pair = lax.ppermute(pair, ("gx", "gy"), across)
+    squares = squares + swap(squares, "gy", 2)
+    pair = jnp.concatenate([pair, swap(pair, "gx", 4)], axis=0)
+    pair = jnp.concatenate([pair, swap(pair, "gx", 2)], axis=0)
+
+    scale = lax.rsqrt(squares.reshape(tokens) / model_width + EPS)[:, None]
     _, position = segment_table(seg_lengths, tokens)
     lane = jnp.arange(HD, dtype=jnp.int32)
     exponent = (lane % (HD // 2)).astype(f32) * (2.0 / HD)
     angle = position.astype(f32)[:, None] * (ROPE_BASE ** (-exponent))[None, :]
     cosine = jnp.cos(angle) * scale
     sine = jnp.where(lane < HD // 2, -1.0, 1.0)[None, :] * jnp.sin(angle) * scale
-    key, value = prepare(own, pair, cosine, sine, jnp.broadcast_to(scale, (tokens, HD)))
-
-    query_blocks = [columns(w_query, (rank ^ r) * piece, piece) for r in range(8)]
-    w_near = jnp.concatenate(query_blocks[0:2], axis=1)
-    w_low = jnp.concatenate(query_blocks[2:4], axis=1)
-    w_cross = jnp.concatenate(query_blocks[4:8], axis=1)
-    w_rows = jnp.concatenate(
-        [lax.dynamic_slice_in_dim(w_out, (rank ^ r) * piece, piece, 0) for r in range(8)], axis=0
-    )
-
-    attended = {}
-    for first in (0, 2):
-        for h in range(2):
-            chunk = jnp.concatenate([parts[first, h], parts[first + 1, h]], axis=0)
-            cross = swap(jnp.dot(chunk, w_cross, preferred_element_type=f32).astype(bf16), "gx", 1)
-            low = jnp.dot(chunk, w_low, preferred_element_type=f32) + cross[:, half_cols // 2 :].astype(f32)
-            near = jnp.dot(chunk, w_near, preferred_element_type=f32) + cross[:, : half_cols // 2].astype(f32)
-            got = swap(low.astype(bf16), "gx", 2)
-            high = near[:, piece:] + got[:, piece:].astype(f32)
-            near = near[:, :piece] + got[:, :piece].astype(f32)
-            query = (near + swap(high.astype(bf16), "gx", 4).astype(f32)).astype(bf16)
-            attended[first, h] = attend(first, h, own, seg_lengths, query, key, value, cosine, sine)
-
+    key, value = prepare(own ^ z_at, pair, cosine, sine, jnp.broadcast_to(scale, (tokens, HD)))
+
+    attended, last = {}, None
+    for first, h in ((0, 0), (0, 1), (2, 0), (2, 1)):
+        cross = crossed_in[first, h]
+        keep = keeps[first][h * rows : (h + 1) * rows]
+        low = (keep[:, 2 * piece :].astype(f32) + cross[:, 2 * piece :].astype(f32)).astype(bf16)
+        if last is not None:
+            low = after(low, last, keeps[2])
+        last = got = swap(low, "gx", 2)
+        near = keep[:, : 2 * piece].astype(f32) + cross[:, : 2 * piece].astype(f32)
+        high = near[:, piece:] + got[:, piece:].astype(f32)
+        near = near[:, :piece] + got[:, :piece].astype(f32)
+        got = swap(high.astype(bf16), "gx", 4)
+        query = (near + got.astype(f32)).astype(bf16)
+        attended[first, h] = attend(first, h, own, seg_lengths, query, key, value, cosine, sine)
+    attended[0, 1] = after(attended[0, 1], got)
+
+    w_rows = reorder(after(rank ^ jnp.arange(8, dtype=jnp.int32), crossed_in[2, 0]), w_out)
     kept, crossed = {}, {}
     for first, h in ((0, 0), (2, 0), (2, 1), (0, 1)):
         a = attended[first, h]
         a = jnp.concatenate([a, swap(a, "gx", 4)], axis=1)
         a = jnp.concatenate([a, swap(a, "gx", 2)], axis=1)
-        a = jnp.concatenate([a, swap(a, "gx", 1)], axis=1)
+        got = swap_x(a)
+        a = jnp.concatenate([a, got], axis=1)
         given = jnp.dot(a[half_rows:], w_rows, preferred_element_type=f32).astype(bf16)
         mine = jnp.dot(a[:half_rows], w_rows, preferred_element_type=f32)
         mine = mine + swap(given, "gy", 1).astype(f32)

time: 464 us -> 384 us (0.83)
  waiting for transfers between devices: 204 us -> 128 us
  blocking collectives: 58.4 us -> 0 us
  Pallas kernels: 11.5 us -> 54.4 us
  other arithmetic: 14 us -> 51.8 us
  matrix products: 69.4 us -> 34.9 us
  between operations: 14.4 us -> 0.99 us
  starting transfers between devices: 42.9 us -> 54.6 us
  local copies, waits for them, and re-layouts: 44.4 us -> 52 us
    ppermute x39 -> x46, waiting for transfers between devices: 204 us -> 128 us  [swap(): lax.ppermute(value, axis, [(i, i ^ bit) for i in range(lax.axis_size(axis...]
    psum x1 -> x0, blocking collectives: 58.4 us -> none  [shards_8x4(): squares = lax.psum(squares, ('gx', 'gy'))]
    dot_general x14 -> x0, matrix products: 49.4 us -> none  [the longest x4 17.9 us: shards_8x4(): jnp.dot(chunk, w_cross, preferred_element_type=f32).astype(bf16)]
    pallas_call x0 -> x26, Pallas kernels: none -> 43.1 us  [the longest x4 34.1 us: project(): pl.pallas_call(functools.partial(project_kernel, len(pieces)), out_shape=...]
    unnamed x72 -> x142, local copies, waits for them, and re-layouts: 32.1 us -> 48.5 us
    convert_element_type x8 -> x10, other arithmetic: 0.84 us -> 14.5 us  [the longest x4 6.38 us: shards_8x4(): got = swap(high.astype(bf16), 'gx', 4)]
    dot_general x4, matrix products: 9.94 us -> 22.9 us  [shards_8x4(): jnp.dot(a[half_rows:], w_rows, preferred_element_type=f32).astype(bf16)]
    ppermute x39 -> x46, starting transfers between devices: 42.9 us -> 53.1 us  [swap(): lax.ppermute(value, axis, [(i, i ^ bit) for i in range(lax.axis_size(axis...]
  transfers between devices with their start and end apart: 40 -> 47, of which waited for: 18 -> 17; matrix products, arithmetic and copies ran while one was open for 26% -> 23% of each run, Pallas kernels for 3% -> 14%
where the time goes in v2:
time: 384 us; the launch traced here: 376 us
  waiting for transfers between devices  128 us (33%)
  starting transfers between devices  54.6 us (14%)
  Pallas kernels  54.4 us (14%)
  local copies, waits for them, and re-layouts  52 us (14%)
  other arithmetic  51.8 us (13%)
  matrix products  34.9 us (9%)
    ppermute x46, waiting for transfers between devices, swap(): lax.ppermute(value, axis, [(i, i ^ bit) for i in range(lax.axis_size(axis...  128 us
    ppermute x46, starting transfers between devices, swap(): lax.ppermute(value, axis, [(i, i ^ bit) for i in range(lax.axis_size(axis...  53.1 us
    unnamed x142, local copies, waits for them, and re-layouts  48.5 us
    pallas_call x4, Pallas kernels, project(): pl.pallas_call(functools.partial(project_kernel, len(pieces)), out_shape=...  34.1 us
    dot_general x4, matrix products, shards_8x4(): jnp.dot(a[half_rows:], w_rows, preferred_element_type=f32).astype(bf16)  22.9 us
    dot_general x4, matrix products, shards_8x4(): mine = jnp.dot(a[:half_rows], w_rows, preferred_element_type=f32)  12 us
    pallas_call x4, Pallas kernels, attend(): pl.pallas_call(functools.partial(attend_kernel, first, half), out_shape=j...  10.9 us
  transfers between devices with their start and end apart: 47, of which 17 were waited for; matrix products, arithmetic and copies ran while one was open for 23% of the time, Pallas kernels for 14%

profile of v2, /device:TPU:0, one launch (start us, length us, event | category | flops | bytes accessed | tf_op | source)
XLA Modules:
  0.0 376.4 jit_solution(4191053104588809335)
XLA Ops:
  11.6 7.4 %shard_map.73 = (bf16[512,1024]{1,0:T(8,128)(2,1)S(1)}, bf16[512,1024]{1,0:T(8,128)(2,1)S(1)}) custom-call(s32[5]{0:T(128)S(1)} %pad_add_fusion.place_ref, f32[1,2048]{1,0:T(1,128)S(1)} %bitcast.23, bf16[512,2048]{1,0:T(8,128)(2,1)S(1)} %copy-done.6, bf16[2048,1024]{1,0:T(8,128)(2,1)S(1)} %copy-done.29, bf16[2048,1024]{1,0:T(8,128)(2,1)S(1)} %copy-done.30), custom_call_target="tpu_custom_call" | custom-call | flops 4294967296 | bytes 8388608 | tf_op jit(solution)/shard_map/pallas_call | solution.py:296
  28.3 8.8 %shard_map.75 = (bf16[512,1024]{1,0:T(8,128)(2,1)S(1)}, bf16[512,1024]{1,0:T(8,128)(2,1)S(1)}) custom-call(s32[4]{0:T(128)S(1)} %copy-done.23, f32[1,2048]{1,0:T(1,128)S(1)} %bitcast.24, bf16[256,2048]{1,0:T(8,128)(2,1)S(1)} %get-tuple-element.34.refs_0_, bf16[256,2048]{1,0:T(8,128)(2,1)} %collective-permute-done.refs_1_, ...), custom_call_target="tpu_custom_call" | custom-call | flops 4294967296 | bytes 10485760 | tf_op jit(solution)/shard_map/pallas_call | solution.py:331
  43.2 8.8 %shard_map.77.refs_1_ = bf16[1024,1024]{1,0:T(8,128)(2,1)S(1)} custom-call(s32[4]{0:T(128)S(1)} %copy-done.21, f32[1,2048]{1,0:T(1,128)S(1)} %bitcast.25, bf16[256,2048]{1,0:T(8,128)(2,1)S(1)} %get-tuple-element.34.refs_0_, bf16[256,2048]{1,0:T(8,128)(2,1)} %collective-permute-done.refs_1_, bf16[256,2048]{1,0:T(8,128)(2,1)} %get-tuple-element.33.refs_2_, ...), custom_call_target="tpu_custom_call" | custom-call | flops 4294967296 | bytes 10485760 | tf_op jit(solution)/shard_map/pallas_call | solution.py:331
  61.2 8.8 %collective-permute-done.18.refs_0_ = bf16[256,2048]{1,0:T(8,128)(2,1)} collective-permute-done((bf16[256,2048]{1,0:T(8,128)(2,1)S(1)}, bf16[256,2048]{1,0:T(8,128)(2,1)}, u32[]{:S(2)}, u32[]{:S(2)}) %collective-permute-start.18) | collective-permute-done | bytes 1048608 | tf_op jit(solution)/shard_map/ppermute | solution.py:144
  74.1 4.2 %collective-permute-done.4.refs_1_ = bf16[512,1024]{1,0:T(8,128)(2,1)} collective-permute-done((bf16[512,1024]{1,0:T(8,128)(2,1)}, bf16[512,1024]{1,0:T(8,128)(2,1)}, u32[]{:S(2)}, u32[]{:S(2)}) %collective-permute-start.4) | collective-permute-done | bytes 1048608 | tf_op jit(solution)/shard_map/ppermute | solution.py:144
  84.0 10.0 %collective-permute-done.14 = f32[16,128]{1,0:T(8,128)S(1)} collective-permute-done((f32[16,128]{1,0:T(8,128)S(1)}, f32[16,128]{1,0:T(8,128)S(1)}, u32[]{:S(2)}, u32[]{:S(2)}) %collective-permute-start.14) | collective-permute-done | bytes 8224 | tf_op jit(solution)/shard_map/ppermute | solution.py:144
  102.9 8.2 %shard_map.85 = (bf16[512,1024]{1,0:T(8,128)(2,1)S(1)}, bf16[512,1024]{1,0:T(8,128)(2,1)S(1)}) custom-call(s32[4]{0:T(128)S(1)} %copy-done.24, f32[1,2048]{1,0:T(1,128)S(1)} %bitcast.26, bf16[256,2048]{1,0:T(8,128)(2,1)} %collective-permute-done.18.refs_0_, bf16[256,2048]{1,0:T(8,128)(2,1)S(1)} %collective-permute-done.19.refs_1_, ...), custom_call_target="tpu_custom_call" | custom-call | flops 4294967296 | bytes 10485760 | tf_op jit(solution)/shard_map/pallas_call | solution.py:331
  118.2 4.0 %collective-permute-start.5 = (bf16[512,512]{1,0:T(8,128)(2,1)}, bf16[512,512]{1,0:T(8,128)(2,1)}, u32[]{:S(2)}, u32[]{:S(2)}) collective-permute-start(bf16[512,512]{1,0:T(8,128)(2,1)} %get-tuple-element.29), channel_id=1, source_target_pairs={{0,8},{4,12},{8,0},{12,4},{16,24},{20,28},{24,16},{28,20},{1,9},{5... | collective-permute-start | bytes 1572872 | tf_op jit(solution)/shard_map/ppermute | solution.py:144
  122.3 3.8 %fusion.8 = (f32[2048,128]{1,0:T(8,128)S(1)}, f32[2048,128]{1,0:T(8,128)S(1)}) fusion(f32[128]{0:T(128)S(1)} %get-tuple-element.37, f32[2048]{0:T(1024)S(1)} %rsqrt_bitcast_fusion, f32[128]{0:T(128)S(1)} %get-tuple-element.38, f32[2048]{0:T(1024)S(1)} %subtract_convert_fusion), kind=kLoop, calls=%fused_computation.25 | loop fusion | flops 1048576 | bytes 2114560 | tf_op jit(solution)/shard_map/mul | solution.py:430
  129.3 7.8 %collective-permute-done.23.refs_1_ = bf16[512,1024]{1,0:T(8,128)(2,1)S(1)} collective-permute-done((bf16[512,1024]{1,0:T(8,128)(2,1)}, bf16[512,1024]{1,0:T(8,128)(2,1)S(1)}, u32[]{:S(2)}, u32[]{:S(2)}) %collective-permute-start.23) | collective-permute-done | bytes 1048608 | tf_op jit(solution)/shard_map/ppermute | solution.py:144
  147.9 8.2 %shard_map.93.refs_2_ = bf16[1024,1024]{1,0:T(8,128)(2,1)S(1)} custom-call(s32[4]{0:T(128)S(1)} %copy-done.19, f32[1,2048]{1,0:T(1,128)S(1)} %bitcast.27, bf16[256,2048]{1,0:T(8,128)(2,1)} %collective-permute-done.18.refs_0_, bf16[256,2048]{1,0:T(8,128)(2,1)S(1)} %copy-done.36, bf16[256,2048]{1,0:T(8,128)(2,1)S(1)} %copy-done.32, ...), custom_call_target="tpu_custom_call" | custom-call | flops 4294967296 | bytes 10485760 | tf_op jit(solution)/shard_map/pallas_call | solution.py:331
  160.4 4.7 %collective-permute-start.27 = (bf16[512,512]{1,0:T(8,128)(2,1)}, bf16[512,512]{1,0:T(8,128)(2,1)}, u32[]{:S(2)}, u32[]{:S(2)}) collective-permute-start(bf16[512,512]{1,0:T(8,128)(2,1)} %shard_map.94), channel_id=1, source_target_pairs={{0,8},{4,12},{8,0},{12,4},{16,24},{20,28},{24,16},{28,20},{1,9},{5... | collective-permute-start | bytes 1572872 | tf_op jit(solution)/shard_map/ppermute | solution.py:144
  170.1 6.3 %collective-permute-done.27.refs_1_ = bf16[512,512]{1,0:T(8,128)(2,1)} collective-permute-done((bf16[512,512]{1,0:T(8,128)(2,1)}, bf16[512,512]{1,0:T(8,128)(2,1)}, u32[]{:S(2)}, u32[]{:S(2)}) %collective-permute-start.27) | collective-permute-done | bytes 524320 | tf_op jit(solution)/shard_map/ppermute | solution.py:144
  186.7 16.3 %collective-permute-done.16 = bf16[512,256]{1,0:T(8,128)(2,1)S(1)} collective-permute-done((bf16[512,256]{1,0:T(8,128)(2,1)S(1)}, bf16[512,256]{1,0:T(8,128)(2,1)S(1)}, u32[]{:S(2)}, u32[]{:S(2)}) %collective-permute-start.16) | collective-permute-done | bytes 262176 | tf_op jit(solution)/shard_map/ppermute | solution.py:144
  218.5 3.8 %collective-permute-done.17 = bf16[512,512]{1,0:T(8,128)(2,1)} collective-permute-done((bf16[512,512]{1,0:T(8,128)(2,1)}, bf16[512,512]{1,0:T(8,128)(2,1)}, u32[]{:S(2)}, u32[]{:S(2)}) %collective-permute-start.17) | collective-permute-done | bytes 524320 | tf_op jit(solution)/shard_map/ppermute | solution.py:144
  225.7 4.8 %collective-permute-done.29 = bf16[512,256]{1,0:T(8,128)(2,1)} collective-permute-done((bf16[512,256]{1,0:T(8,128)(2,1)}, bf16[512,256]{1,0:T(8,128)(2,1)}, u32[]{:S(2)}, u32[]{:S(2)}) %collective-permute-start.29) | collective-permute-done | bytes 262176 | tf_op jit(solution)/shard_map/ppermute | solution.py:144
  247.2 10.8 %collective-permute-done.37.refs_1_ = bf16[512,256]{1,0:T(8,128)(2,1)S(1)} collective-permute-done((bf16[512,256]{1,0:T(8,128)(2,1)S(1)}, bf16[512,256]{1,0:T(8,128)(2,1)S(1)}, u32[]{:S(2)}, u32[]{:S(2)}) %collective-permute-start.37) | collective-permute-done | bytes 262176 | tf_op jit(solution)/shard_map/ppermute | solution.py:144
  272.3 7.0 %convolution_convert_fusion.3 = bf16[256,2048]{1,0:T(8,128)(2,1)} fusion(bf16[2048,2048]{1,0:T(8,128)(2,1)} %copy-done.3, bf16[512,2048]{1,0:T(8,128)(2,1)} %pad_maximum_fusion), kind=kOutput, calls=%fused_computation.14 | convolution fusion | flops 2148007936 | bytes 10485760 | tf_op jit(solution)/shard_map/dot_general | solution.py:457
  289.6 7.7 %convolution_convert_fusion.2 = bf16[256,2048]{1,0:T(8,128)(2,1)} fusion(bf16[2048,2048]{1,0:T(8,128)(2,1)} %copy-done.3, bf16[512,2048]{1,0:T(8,128)(2,1)S(1)} %pad_maximum_fusion.1), kind=kOutput, calls=%fused_computation.13 | convolution fusion | flops 2148007936 | bytes 10485760 | tf_op jit(solution)/shard_map/dot_general | solution.py:457
  298.4 12.2 %collective-permute-done.42.refs_1_ = bf16[512,1024]{1,0:T(8,128)(2,1)S(1)} collective-permute-done((bf16[512,1024]{1,0:T(8,128)(2,1)}, bf16[512,1024]{1,0:T(8,128)(2,1)S(1)}, u32[]{:S(2)}, u32[]{:S(2)}) %collective-permute-start.42) | collective-permute-done | bytes 1048608 | tf_op jit(solution)/shard_map/ppermute | solution.py:144
  314.5 5.9 %convolution_convert_fusion = bf16[256,2048]{1,0:T(8,128)(2,1)S(1)} fusion(bf16[2048,2048]{1,0:T(8,128)(2,1)} %copy-done.3, bf16[512,2048]{1,0:T(8,128)(2,1)S(1)} %pad_maximum_fusion.3), kind=kOutput, calls=%fused_computation.11 | convolution fusion | flops 2148007936 | bytes 10485760 | tf_op jit(solution)/shard_map/dot_general | solution.py:457
  325.7 8.8 %collective-permute-done.43 = bf16[512,1024]{1,0:T(8,128)(2,1)S(1)} collective-permute-done((bf16[512,1024]{1,0:T(8,128)(2,1)}, bf16[512,1024]{1,0:T(8,128)(2,1)S(1)}, u32[]{:S(2)}, u32[]{:S(2)}) %collective-permute-start.43) | collective-permute-done | bytes 1048608 | tf_op jit(solution)/shard_map/ppermute | solution.py:144
  341.1 9.1 %collective-permute-done.34 = bf16[256,2048]{1,0:T(8,128)(2,1)S(1)} collective-permute-done((bf16[256,2048]{1,0:T(8,128)(2,1)S(1)}, bf16[256,2048]{1,0:T(8,128)(2,1)S(1)}, u32[]{:S(2)}, u32[]{:S(2)}) %collective-permute-start.34) | collective-permute-done | bytes 1048608 | tf_op jit(solution)/shard_map/ppermute | solution.py:144
  353.8 18.4 %collective-permute-done.46 = bf16[256,2048]{1,0:T(8,128)(2,1)S(1)} collective-permute-done((bf16[256,2048]{1,0:T(8,128)(2,1)S(1)}, bf16[256,2048]{1,0:T(8,128)(2,1)S(1)}, u32[]{:S(2)}, u32[]{:S(2)}) %collective-permute-start.46) | collective-permute-done | bytes 1048608 | tf_op jit(solution)/shard_map/ppermute | solution.py:144
  (303 shorter events, 179.6 us)
Async XLA Ops:
  22.1 31.2 %collective-permute-start.3 = (bf16[512,1024]{1,0:T(8,128)(2,1)}, bf16[512,1024]{1,0:T(8,128)(2,1)}, u32[]{:S(2)}, u32[]{:S(2)}) collective-permute-start(bf16[512,1024]{1,0:T(8,128)(2,1)} %shard_map.78), channel_id=1, source_target_pairs={{0,4},{4,0},{8,12},{12,8},{16,20},{20,16},{24,28},{28,24},{1,5},{5... | collective-permute-start | bytes 3145736 | tf_op jit(solution)/shard_map/ppermute | solution.py:144
  22.1 38.5 %collective-permute-start.20 = (bf16[256,2048]{1,0:T(8,128)(2,1)}, bf16[256,2048]{1,0:T(8,128)(2,1)S(1)}, u32[]{:S(2)}, u32[]{:S(2)}) collective-permute-start(bf16[256,2048]{1,0:T(8,128)(2,1)} %get-tuple-element.33.refs_2_), channel_id=1, source_target_pairs={{0,2},{1,3},{2,0},{3,1},{4,6},{5,7},{6,4},{7,5},{8,10},{9,11},{10,... | collective-permute-start | bytes 3145736 | tf_op jit(solution)/shard_map/ppermute | solution.py:144
  24.1 45.8 %collective-permute-start.18 = (bf16[256,2048]{1,0:T(8,128)(2,1)S(1)}, bf16[256,2048]{1,0:T(8,128)(2,1)}, u32[]{:S(2)}, u32[]{:S(2)}) collective-permute-start(bf16[256,2048]{1,0:T(8,128)(2,1)S(1)} %get-tuple-element.34.refs_0_), channel_id=1, source_target_pairs={{0,2},{1,3},{2,0},{3,1},{4,6},{5,7},{6,4},{7,5},{8,10},{9,11},{10,... | collective-permute-start | bytes 3145736 | tf_op jit(solution)/shard_map/ppermute | solution.py:144
  53.4 24.9 %collective-permute-start.4 = (bf16[512,1024]{1,0:T(8,128)(2,1)}, bf16[512,1024]{1,0:T(8,128)(2,1)}, u32[]{:S(2)}, u32[]{:S(2)}) collective-permute-start(bf16[512,1024]{1,0:T(8,128)(2,1)} %shard_map.79), channel_id=1, source_target_pairs={{0,4},{4,0},{8,12},{12,8},{16,20},{20,16},{24,28},{28,24},{1,5},{5... | collective-permute-start | bytes 3145736 | tf_op jit(solution)/shard_map/ppermute | solution.py:144
  60.6 38.2 %collective-permute-start.21 = (bf16[256,2048]{1,0:T(8,128)(2,1)S(1)}, bf16[256,2048]{1,0:T(8,128)(2,1)S(1)}, u32[]{:S(2)}, u32[]{:S(2)}) collective-permute-start(bf16[256,2048]{1,0:T(8,128)(2,1)S(1)} %collective-permute-done.20.refs_2_), channel_id=1, source_target_pairs={{0,1},{1,0},{2,3},{3,2},{4,5},{5,4},{6,7},{7,6},{8,9},{9,8},{10,11... | collective-permute-start | bytes 3145736 | tf_op jit(solution)/shard_map/ppermute | solution.py:144
  70.0 28.9 %collective-permute-start.19 = (bf16[256,2048]{1,0:T(8,128)(2,1)}, bf16[256,2048]{1,0:T(8,128)(2,1)S(1)}, u32[]{:S(2)}, u32[]{:S(2)}) collective-permute-start(bf16[256,2048]{1,0:T(8,128)(2,1)} %collective-permute-done.18.refs_0_), channel_id=1, source_target_pairs={{0,1},{1,0},{2,3},{3,2},{4,5},{5,4},{6,7},{7,6},{8,9},{9,8},{10,11... | collective-permute-start | bytes 3145736 | tf_op jit(solution)/shard_map/ppermute | solution.py:144
  78.2 34.8 %collective-permute-start.22 = (bf16[512,1024]{1,0:T(8,128)(2,1)}, bf16[512,1024]{1,0:T(8,128)(2,1)}, u32[]{:S(2)}, u32[]{:S(2)}) collective-permute-start(bf16[512,1024]{1,0:T(8,128)(2,1)} %shard_map.86), channel_id=1, source_target_pairs={{0,4},{4,0},{8,12},{12,8},{16,20},{20,16},{24,28},{28,24},{1,5},{5... | collective-permute-start | bytes 3145736 | tf_op jit(solution)/shard_map/ppermute | solution.py:144
  113.0 24.1 %collective-permute-start.23 = (bf16[512,1024]{1,0:T(8,128)(2,1)}, bf16[512,1024]{1,0:T(8,128)(2,1)S(1)}, u32[]{:S(2)}, u32[]{:S(2)}) collective-permute-start(bf16[512,1024]{1,0:T(8,128)(2,1)} %shard_map.87), channel_id=1, source_target_pairs={{0,4},{4,0},{8,12},{12,8},{16,20},{20,16},{24,28},{28,24},{1,5},{5... | collective-permute-start | bytes 3145736 | tf_op jit(solution)/shard_map/ppermute | solution.py:144
  118.2 20.4 %collective-permute-start.5 = (bf16[512,512]{1,0:T(8,128)(2,1)}, bf16[512,512]{1,0:T(8,128)(2,1)}, u32[]{:S(2)}, u32[]{:S(2)}) collective-permute-start(bf16[512,512]{1,0:T(8,128)(2,1)} %get-tuple-element.29), channel_id=1, source_target_pairs={{0,8},{4,12},{8,0},{12,4},{16,24},{20,28},{24,16},{28,20},{1,9},{5... | collective-permute-start | bytes 1572872 | tf_op jit(solution)/shard_map/ppermute | solution.py:144
  129.3 26.8 %collective-permute-start.11 = (bf16[1024,256]{1,0:T(8,128)(2,1)}, bf16[1024,256]{1,0:T(8,128)(2,1)}, u32[]{:S(2)}, u32[]{:S(2)}) collective-permute-start(bf16[1024,256]{1,0:T(8,128)(2,1)} %pad_maximum_fusion.10), channel_id=1, source_target_pairs={{0,8},{4,12},{8,0},{12,4},{16,24},{20,28},{24,16},{28,20},{1,9},{5... | collective-permute-start | bytes 1572872 | tf_op jit(solution)/shard_map/ppermute | solution.py:144
  138.1 28.3 %collective-permute-start.24 = (bf16[512,1024]{1,0:T(8,128)(2,1)}, bf16[512,1024]{1,0:T(8,128)(2,1)}, u32[]{:S(2)}, u32[]{:S(2)}) collective-permute-start(bf16[512,1024]{1,0:T(8,128)(2,1)} %shard_map.88), channel_id=1, source_target_pairs={{0,4},{4,0},{8,12},{12,8},{16,20},{20,16},{24,28},{28,24},{1,5},{5... | collective-permute-start | bytes 3145736 | tf_op jit(solution)/shard_map/ppermute | solution.py:144
  140.5 24.6 %collective-permute-start.6 = (bf16[512,256]{1,0:T(8,128)(2,1)}, bf16[512,256]{1,0:T(8,128)(2,1)}, u32[]{:S(2)}, u32[]{:S(2)}) collective-permute-start(bf16[512,256]{1,0:T(8,128)(2,1)} %fusion.26), channel_id=1, source_target_pairs={{0,16},{4,20},{8,24},{12,28},{16,0},{20,4},{24,8},{28,12},{1,17},{... | collective-permute-start | bytes 786440 | tf_op jit(solution)/shard_map/ppermute | solution.py:144
  176.4 37.0 %collective-permute-start.28 = (bf16[512,512]{1,0:T(8,128)(2,1)}, bf16[512,512]{1,0:T(8,128)(2,1)}, u32[]{:S(2)}, u32[]{:S(2)}) collective-permute-start(bf16[512,512]{1,0:T(8,128)(2,1)} %shard_map.95), channel_id=1, source_target_pairs={{0,8},{4,12},{8,0},{12,4},{16,24},{20,28},{24,16},{28,20},{1,9},{5... | collective-permute-start | bytes 1572872 | tf_op jit(solution)/shard_map/ppermute | solution.py:144
  182.0 21.1 %collective-permute-start.16 = (bf16[512,256]{1,0:T(8,128)(2,1)S(1)}, bf16[512,256]{1,0:T(8,128)(2,1)S(1)}, u32[]{:S(2)}, u32[]{:S(2)}) collective-permute-start(bf16[512,256]{1,0:T(8,128)(2,1)S(1)} %shard_map.83), channel_id=1, source_target_pairs={{0,16},{4,20},{8,24},{12,28},{16,0},{20,4},{24,8},{28,12},{1,17},{... | collective-permute-start | bytes 786440 | tf_op jit(solution)/shard_map/ppermute | solution.py:144
  184.1 31.1 %collective-permute-start.35 = (bf16[512,256]{1,0:T(8,128)(2,1)}, bf16[512,256]{1,0:T(8,128)(2,1)}, u32[]{:S(2)}, u32[]{:S(2)}) collective-permute-start(bf16[512,256]{1,0:T(8,128)(2,1)} %fusion.20), channel_id=1, source_target_pairs={{0,16},{4,20},{8,24},{12,28},{16,0},{20,4},{24,8},{28,12},{1,17},{... | collective-permute-start | bytes 786440 | tf_op jit(solution)/shard_map/ppermute | solution.py:144
  224.4 37.7 %collective-permute-start.25 = (bf16[512,1024]{1,0:T(8,128)(2,1)}, bf16[512,1024]{1,0:T(8,128)(2,1)S(1)}, u32[]{:S(2)}, u32[]{:S(2)}) collective-permute-start(bf16[512,1024]{1,0:T(8,128)(2,1)} %shard_map.89), channel_id=1, source_target_pairs={{0,4},{4,0},{8,12},{12,8},{16,20},{20,16},{24,28},{28,24},{1,5},{5... | collective-permute-start | bytes 3145736 | tf_op jit(solution)/shard_map/ppermute | solution.py:144
  236.8 21.3 %collective-permute-start.37 = (bf16[512,256]{1,0:T(8,128)(2,1)S(1)}, bf16[512,256]{1,0:T(8,128)(2,1)S(1)}, u32[]{:S(2)}, u32[]{:S(2)}) collective-permute-start(bf16[512,256]{1,0:T(8,128)(2,1)S(1)} %fusion.19), channel_id=1, source_target_pairs={{0,16},{4,20},{8,24},{12,28},{16,0},{20,4},{24,8},{28,12},{1,17},{... | collective-permute-start | bytes 786440 | tf_op jit(solution)/shard_map/ppermute | solution.py:144
  247.2 21.4 %collective-permute-start.31 = (bf16[512,512]{1,0:T(8,128)(2,1)}, bf16[512,512]{1,0:T(8,128)(2,1)}, u32[]{:S(2)}, u32[]{:S(2)}) collective-permute-start(bf16[512,512]{1,0:T(8,128)(2,1)} %pad_maximum_fusion.12), channel_id=1, source_target_pairs={{0,8},{4,12},{8,0},{12,4},{16,24},{20,28},{24,16},{28,20},{1,9},{5... | collective-permute-start | bytes 1572872 | tf_op jit(solution)/shard_map/ppermute | solution.py:144
  279.3 61.7 %collective-permute-start.26 = (bf16[256,2048]{1,0:T(8,128)(2,1)}, bf16[256,2048]{1,0:T(8,128)(2,1)}, u32[]{:S(2)}, u32[]{:S(2)}) collective-permute-start(bf16[256,2048]{1,0:T(8,128)(2,1)} %convolution_convert_fusion.3), channel_id=1, source_target_pairs={{0,1},{1,0},{2,3},{3,2},{4,5},{5,4},{6,7},{7,6},{8,9},{9,8},{10,11... | collective-permute-start | bytes 3145736 | tf_op jit(solution)/shard_map/ppermute | solution.py:144
  286.7 23.9 %collective-permute-start.42 = (bf16[512,1024]{1,0:T(8,128)(2,1)}, bf16[512,1024]{1,0:T(8,128)(2,1)S(1)}, u32[]{:S(2)}, u32[]{:S(2)}) collective-permute-start(bf16[512,1024]{1,0:T(8,128)(2,1)} %shard_map.102), channel_id=1, source_target_pairs={{0,4},{4,0},{8,12},{12,8},{16,20},{20,16},{24,28},{28,24},{1,5},{5... | collective-permute-start | bytes 3145736 | tf_op jit(solution)/shard_map/ppermute | solution.py:144
  297.2 23.3 %collective-permute-start.33 = (bf16[256,2048]{1,0:T(8,128)(2,1)}, bf16[256,2048]{1,0:T(8,128)(2,1)}, u32[]{:S(2)}, u32[]{:S(2)}) collective-permute-start(bf16[256,2048]{1,0:T(8,128)(2,1)} %convolution_convert_fusion.2), channel_id=1, source_target_pairs={{0,1},{1,0},{2,3},{3,2},{4,5},{5,4},{6,7},{7,6},{8,9},{9,8},{10,11... | collective-permute-start | bytes 3145736 | tf_op jit(solution)/shard_map/ppermute | solution.py:144
  311.5 23.0 %collective-permute-start.43 = (bf16[512,1024]{1,0:T(8,128)(2,1)}, bf16[512,1024]{1,0:T(8,128)(2,1)S(1)}, u32[]{:S(2)}, u32[]{:S(2)}) collective-permute-start(bf16[512,1024]{1,0:T(8,128)(2,1)} %shard_map.103), channel_id=1, source_target_pairs={{0,4},{4,0},{8,12},{12,8},{16,20},{20,16},{24,28},{28,24},{1,5},{5... | collective-permute-start | bytes 3145736 | tf_op jit(solution)/shard_map/ppermute | solution.py:144
  324.1 26.0 %collective-permute-start.34 = (bf16[256,2048]{1,0:T(8,128)(2,1)S(1)}, bf16[256,2048]{1,0:T(8,128)(2,1)S(1)}, u32[]{:S(2)}, u32[]{:S(2)}) collective-permute-start(bf16[256,2048]{1,0:T(8,128)(2,1)S(1)} %fusion.2), channel_id=1, source_target_pairs={{0,2},{1,3},{2,0},{3,1},{4,6},{5,7},{6,4},{7,5},{8,10},{9,11},{10,... | collective-permute-start | bytes 3145736 | tf_op jit(solution)/shard_map/ppermute | solution.py:144
  339.5 32.7 %collective-permute-start.46 = (bf16[256,2048]{1,0:T(8,128)(2,1)S(1)}, bf16[256,2048]{1,0:T(8,128)(2,1)S(1)}, u32[]{:S(2)}, u32[]{:S(2)}) collective-permute-start(bf16[256,2048]{1,0:T(8,128)(2,1)S(1)} %fusion.3), channel_id=1, source_target_pairs={{0,2},{1,3},{2,0},{3,1},{4,6},{5,7},{6,4},{7,5},{8,10},{9,11},{10,... | collective-permute-start | bytes 3145736 | tf_op jit(solution)/shard_map/ppermute | solution.py:144
  (93 other events, 680.6 us)

commit v3 on v2

--- a/solution.py
+++ b/solution.py
@@ -383,9 +383,9 @@
 
     x_served = []
 
-    def swap_x(value):
+    def swap_x(value, *others):
         if x_served:
-            value = after(value, x_served[-1])
+            value = after(value, x_served[-1], *others)
         x_served.append(swap(value, "gx", 1))
         return x_served[-1]
 
@@ -428,37 +428,66 @@
     angle = position.astype(f32)[:, None] * (ROPE_BASE ** (-exponent))[None, :]
     cosine = jnp.cos(angle) * scale
     sine = jnp.where(lane < HD // 2, -1.0, 1.0)[None, :] * jnp.sin(angle) * scale
-    key, value = prepare(own ^ z_at, pair, cosine, sine, jnp.broadcast_to(scale, (tokens, HD)))
-
-    attended, last = {}, None
-    for first, h in ((0, 0), (0, 1), (2, 0), (2, 1)):
+
+    served, sums, halved, attended, gathered = [], {}, {}, {}, {}
+
+    def halve_near(first, h, *others):
         cross = crossed_in[first, h]
         keep = keeps[first][h * rows : (h + 1) * rows]
         low = (keep[:, 2 * piece :].astype(f32) + cross[:, 2 * piece :].astype(f32)).astype(bf16)
-        if last is not None:
-            low = after(low, last, keeps[2])
-        last = got = swap(low, "gx", 2)
+        if served:
+            low = after(low, served[-1], *others)
+        served.append(swap(low, "gx", 2))
         near = keep[:, : 2 * piece].astype(f32) + cross[:, : 2 * piece].astype(f32)
+        sums[first, h] = near, served[-1]
+
+    def halve_far(first, h, *others):
+        near, got = sums[first, h]
+        if others:
+            got = after(got, *others)
         high = near[:, piece:] + got[:, piece:].astype(f32)
         near = near[:, :piece] + got[:, :piece].astype(f32)
-        got = swap(high.astype(bf16), "gx", 4)
+        halved[first, h] = near, swap(high.astype(bf16), "gx", 4)
+
+    def attend_chunk(first, h):
+        near, got = halved[first, h]
         query = (near + got.astype(f32)).astype(bf16)
         attended[first, h] = attend(first, h, own, seg_lengths, query, key, value, cosine, sine)
+
+    halve_near(0, 0)
+    halve_far(0, 0)
+    halve_near(0, 1)
+    pair = after(pair, served[-1])
+    key, value = prepare(own ^ z_at, pair, cosine, sine, jnp.broadcast_to(scale, (tokens, HD)))
+    attend_chunk(0, 0)
+    gathered[0, 0] = swap(attended[0, 0], "gx", 4)
+    halve_near(2, 0, gathered[0, 0])
+    wide = jnp.concatenate([attended[0, 0], gathered[0, 0]], axis=1)
+    halve_far(2, 0, wide)
+    attend_chunk(2, 0)
+    halve_far(0, 1)
+    attend_chunk(0, 1)
+    halve_near(2, 1)
+    halve_far(2, 1)
+    attend_chunk(2, 1)
+    got = halved[2, 1][1]
     attended[0, 1] = after(attended[0, 1], got)
 
     w_rows = reorder(after(rank ^ jnp.arange(8, dtype=jnp.int32), crossed_in[2, 0]), w_out)
     kept, crossed = {}, {}
+    mine_given = {}
     for first, h in ((0, 0), (2, 0), (2, 1), (0, 1)):
         a = attended[first, h]
-        a = jnp.concatenate([a, swap(a, "gx", 4)], axis=1)
+        a = wide if (first, h) in gathered else jnp.concatenate([a, swap(a, "gx", 4)], axis=1)
         a = jnp.concatenate([a, swap(a, "gx", 2)], axis=1)
-        got = swap_x(a)
+        got = swap_x(a, *([mine_given[0]] if (first, h) == (0, 1) else []))
         a = jnp.concatenate([a, got], axis=1)
         given = jnp.dot(a[half_rows:], w_rows, preferred_element_type=f32).astype(bf16)
         mine = jnp.dot(a[:half_rows], w_rows, preferred_element_type=f32)
         mine = mine + swap(given, "gy", 1).astype(f32)
         if first:
-            crossed[h] = swap(mine.astype(bf16), "gy", 2)
+            mine_given[h] = mine.astype(bf16)
+            crossed[h] = swap(mine_given[h], "gy", 2)
         else:
             kept[h] = mine
     return jnp.concatenate(

time: 384 us -> 403 us (1.049)
  waiting for transfers between devices: 128 us -> 158 us
  local copies, waits for them, and re-layouts: 52 us -> 45.9 us
    ppermute x46, waiting for transfers between devices: 128 us -> 158 us  [swap(): lax.ppermute(value, axis, [(i, i ^ bit) for i in range(lax.axis_size(axis...]
    unnamed x142, local copies, waits for them, and re-layouts: 48.5 us -> 43.3 us
    dot_general x4, matrix products: 22.9 us -> 18.2 us  [shards_8x4(): jnp.dot(a[half_rows:], w_rows, preferred_element_type=f32).astype(bf16)]
  transfers between devices with their start and end apart: 47 -> 47, of which waited for: 17 -> 24; matrix products, arithmetic and copies ran while one was open for 23% -> 20% of each run, Pallas kernels for 14% -> 14%
where the time goes in v3:
time: 403 us; the launch traced here: 396 us
  waiting for transfers between devices  158 us (39%)
  Pallas kernels  54.7 us (14%)
  other arithmetic  52.1 us (13%)
  starting transfers between devices  51.9 us (13%)
  local copies, waits for them, and re-layouts  45.9 us (11%)
  matrix products  32.5 us (8%)
    ppermute x46, waiting for transfers between devices, swap(): lax.ppermute(value, axis, [(i, i ^ bit) for i in range(lax.axis_size(axis...  158 us
    ppermute x46, starting transfers between devices, swap(): lax.ppermute(value, axis, [(i, i ^ bit) for i in range(lax.axis_size(axis...  50 us
    unnamed x142, local copies, waits for them, and re-layouts  43.3 us
    pallas_call x4, Pallas kernels, project(): pl.pallas_call(functools.partial(project_kernel, len(pieces)), out_shape=...  34.6 us
    dot_general x4, matrix products, shards_8x4(): jnp.dot(a[half_rows:], w_rows, preferred_element_type=f32).astype(bf16)  18.2 us
    dot_general x4, matrix products, shards_8x4(): mine = jnp.dot(a[:half_rows], w_rows, preferred_element_type=f32)  14.2 us
    pallas_call x4, Pallas kernels, attend(): pl.pallas_call(functools.partial(attend_kernel, first, half), out_shape=j...  10.9 us
  transfers between devices with their start and end apart: 47, of which 24 were waited for; matrix products, arithmetic and copies ran while one was open for 20% of the time, Pallas kernels for 14%

profile of v3, /device:TPU:0, one launch (start us, length us, event | category | flops | bytes accessed | tf_op | source)
XLA Modules:
  0.0 395.8 jit_solution(9814843178263307773)
XLA Ops:
  11.6 7.4 %shard_map.73 = (bf16[512,1024]{1,0:T(8,128)(2,1)S(1)}, bf16[512,1024]{1,0:T(8,128)(2,1)S(1)}) custom-call(s32[5]{0:T(128)S(1)} %pad_add_fusion.place_ref, f32[1,2048]{1,0:T(1,128)S(1)} %bitcast.23, bf16[512,2048]{1,0:T(8,128)(2,1)S(1)} %copy-done.5, bf16[2048,1024]{1,0:T(8,128)(2,1)S(1)} %copy-done.28, bf16[2048,1024]{1,0:T(8,128)(2,1)S(1)} %copy-done.29), custom_call_target="tpu_custom_call" | custom-call | flops 4294967296 | bytes 8388608 | tf_op jit(solution)/shard_map/pallas_call | solution.py:296
  28.1 8.8 %shard_map.75 = (bf16[512,1024]{1,0:T(8,128)(2,1)S(1)}, bf16[512,1024]{1,0:T(8,128)(2,1)S(1)}) custom-call(s32[4]{0:T(128)S(1)} %copy-done.22, f32[1,2048]{1,0:T(1,128)S(1)} %bitcast.24, bf16[256,2048]{1,0:T(8,128)(2,1)S(1)} %get-tuple-element.34.refs_0_, bf16[256,2048]{1,0:T(8,128)(2,1)} %collective-permute-done.refs_1_, ...), custom_call_target="tpu_custom_call" | custom-call | flops 4294967296 | bytes 10485760 | tf_op jit(solution)/shard_map/pallas_call | solution.py:331
  43.0 8.8 %shard_map.77.refs_1_ = bf16[1024,1024]{1,0:T(8,128)(2,1)S(1)} custom-call(s32[4]{0:T(128)S(1)} %copy-done.20, f32[1,2048]{1,0:T(1,128)S(1)} %bitcast.25, bf16[256,2048]{1,0:T(8,128)(2,1)S(1)} %get-tuple-element.34.refs_0_, bf16[256,2048]{1,0:T(8,128)(2,1)} %collective-permute-done.refs_1_, bf16[256,2048]{1,0:T(8,128)(2,1)} %get-tuple-element.33.refs_2_, ...), custom_call_target="tpu_custom_call" | custom-call | flops 4294967296 | bytes 10485760 | tf_op jit(solution)/shard_map/pallas_call | solution.py:331
  62.1 7.9 %collective-permute-done.20.refs_0_ = bf16[256,2048]{1,0:T(8,128)(2,1)} collective-permute-done((bf16[256,2048]{1,0:T(8,128)(2,1)S(1)}, bf16[256,2048]{1,0:T(8,128)(2,1)}, u32[]{:S(2)}, u32[]{:S(2)}) %collective-permute-start.20) | collective-permute-done | bytes 1048608 | tf_op jit(solution)/shard_map/ppermute | solution.py:144
  79.8 8.2 %collective-permute-done.16 = f32[16,128]{1,0:T(8,128)S(1)} collective-permute-done((f32[16,128]{1,0:T(8,128)S(1)}, f32[16,128]{1,0:T(8,128)S(1)}, u32[]{:S(2)}, u32[]{:S(2)}) %collective-permute-start.16) | collective-permute-done | bytes 8224 | tf_op jit(solution)/shard_map/ppermute | solution.py:144
  99.1 8.2 %shard_map.88 = (bf16[512,1024]{1,0:T(8,128)(2,1)S(1)}, bf16[512,1024]{1,0:T(8,128)(2,1)S(1)}) custom-call(s32[4]{0:T(128)S(1)} %copy-done.23, f32[1,2048]{1,0:T(1,128)S(1)} %bitcast.26, bf16[256,2048]{1,0:T(8,128)(2,1)} %collective-permute-done.20.refs_0_, bf16[256,2048]{1,0:T(8,128)(2,1)S(1)} %collective-permute-done.21.refs_1_, ...), custom_call_target="tpu_custom_call" | custom-call | flops 4294967296 | bytes 10485760 | tf_op jit(solution)/shard_map/pallas_call | solution.py:331
  114.2 4.0 collective-permute-start.5
  124.3 9.0 %collective-permute-done.5.refs_1_ = bf16[512,512]{1,0:T(8,128)(2,1)S(1)} collective-permute-done((bf16[512,512]{1,0:T(8,128)(2,1)S(1)}, bf16[512,512]{1,0:T(8,128)(2,1)S(1)}, u32[]{:S(2)}, u32[]{:S(2)}) %collective-permute-start.5) | collective-permute-done | bytes 524320 | tf_op jit(solution)/shard_map/ppermute | solution.py:144
  145.0 8.7 %shard_map.95 = bf16[1024,1024]{1,0:T(8,128)(2,1)S(1)} custom-call(s32[4]{0:T(128)S(1)} %copy-done.18, f32[1,2048]{1,0:T(1,128)S(1)} %bitcast.27, bf16[256,2048]{1,0:T(8,128)(2,1)} %collective-permute-done.20.refs_0_, bf16[256,2048]{1,0:T(8,128)(2,1)S(1)} %copy-done.35, bf16[256,2048]{1,0:T(8,128)(2,1)S(1)} %copy-done.31, bf16[256,2048]{1,0:T(8,128)(2,1)S(1)} %copy-done.33, ...), custom_call_target="tpu_custom_call" | custom-call | flops 4294967296 | bytes 10485760 | tf_op jit(solution)/shard_map/pallas_call | solution.py:331
  170.8 8.9 %collective-permute-done.18.refs_2_ = bf16[512,256]{1,0:T(8,128)(2,1)S(1)} collective-permute-done((bf16[512,256]{1,0:T(8,128)(2,1)S(1)}, bf16[512,256]{1,0:T(8,128)(2,1)S(1)}, u32[]{:S(2)}, u32[]{:S(2)}) %collective-permute-start.18) | collective-permute-done | bytes 262176 | tf_op jit(solution)/shard_map/ppermute | solution.py:144
  182.5 10.5 %collective-permute-done.28.refs_0_.refs_1_ = bf16[512,512]{1,0:T(8,128)(2,1)S(1)} collective-permute-done((bf16[512,512]{1,0:T(8,128)(2,1)}, bf16[512,512]{1,0:T(8,128)(2,1)S(1)}, u32[]{:S(2)}, u32[]{:S(2)}) %collective-permute-start.28) | collective-permute-done | bytes 524320 | tf_op jit(solution)/shard_map/ppermute | solution.py:144
  200.3 10.0 %collective-permute-done.29 = bf16[512,256]{1,0:T(8,128)(2,1)S(1)} collective-permute-done((bf16[512,256]{1,0:T(8,128)(2,1)S(1)}, bf16[512,256]{1,0:T(8,128)(2,1)S(1)}, u32[]{:S(2)}, u32[]{:S(2)}) %collective-permute-start.29) | collective-permute-done | bytes 262176 | tf_op jit(solution)/shard_map/ppermute | solution.py:144
  222.2 5.9 %collective-permute-done.30 = bf16[512,256]{1,0:T(8,128)(2,1)S(1)} collective-permute-done((bf16[512,256]{1,0:T(8,128)(2,1)S(1)}, bf16[512,256]{1,0:T(8,128)(2,1)S(1)}, u32[]{:S(2)}, u32[]{:S(2)}) %collective-permute-start.30) | collective-permute-done | bytes 262176 | tf_op jit(solution)/shard_map/ppermute | solution.py:144
  228.9 10.0 %collective-permute-done.36 = bf16[512,512]{1,0:T(8,128)(2,1)S(1)} collective-permute-done((bf16[512,512]{1,0:T(8,128)(2,1)}, bf16[512,512]{1,0:T(8,128)(2,1)S(1)}, u32[]{:S(2)}, u32[]{:S(2)}) %collective-permute-start.36) | collective-permute-done | bytes 524320 | tf_op jit(solution)/shard_map/ppermute | solution.py:144
  242.2 10.3 %collective-permute-done.31 = bf16[512,512]{1,0:T(8,128)(2,1)S(1)} collective-permute-done((bf16[512,512]{1,0:T(8,128)(2,1)S(1)}, bf16[512,512]{1,0:T(8,128)(2,1)S(1)}, u32[]{:S(2)}, u32[]{:S(2)}) %collective-permute-start.31) | collective-permute-done | bytes 524320 | tf_op jit(solution)/shard_map/ppermute | solution.py:144
  278.1 9.8 %collective-permute-done.40 = bf16[512,256]{1,0:T(8,128)(2,1)} collective-permute-done((bf16[512,256]{1,0:T(8,128)(2,1)S(1)}, bf16[512,256]{1,0:T(8,128)(2,1)}, u32[]{:S(2)}, u32[]{:S(2)}) %collective-permute-start.40) | collective-permute-done | bytes 262176 | tf_op jit(solution)/shard_map/ppermute | solution.py:144
  290.5 7.5 %convolution_convert_fusion.2 = bf16[256,2048]{1,0:T(8,128)(2,1)} fusion(bf16[2048,2048]{1,0:T(8,128)(2,1)} %copy-done.2, bf16[512,2048]{1,0:T(8,128)(2,1)S(1)} %pad_maximum_fusion.1), kind=kOutput, calls=%fused_computation.13 | convolution fusion | flops 2148007936 | bytes 10485760 | tf_op jit(solution)/shard_map/dot_general | solution.py:485
  310.5 4.3 %collective-permute-done.39 = bf16[512,512]{1,0:T(8,128)(2,1)S(1)} collective-permute-done((bf16[512,512]{1,0:T(8,128)(2,1)}, bf16[512,512]{1,0:T(8,128)(2,1)S(1)}, u32[]{:S(2)}, u32[]{:S(2)}) %collective-permute-start.39) | collective-permute-done | bytes 524320 | tf_op jit(solution)/shard_map/ppermute | solution.py:144
  315.9 7.0 %fusion.2.refs_2_ = bf16[256,2048]{1,0:T(8,128)(2,1)} fusion(bf16[2048,2048]{1,0:T(8,128)(2,1)} %copy-done.2, bf16[256,2048]{1,0:T(8,128)(2,1)} %collective-permute-done.33, bf16[512,2048]{1,0:T(8,128)(2,1)S(1)} %copy-done.57), kind=kOutput, calls=%fused_computation.7 | convolution fusion | flops 2149056512 | bytes 11534336 | tf_op jit(solution)/shard_map/dot_general | solution.py:486
  322.9 8.2 %collective-permute-done.42.refs_1_ = bf16[512,1024]{1,0:T(8,128)(2,1)S(1)} collective-permute-done((bf16[512,1024]{1,0:T(8,128)(2,1)}, bf16[512,1024]{1,0:T(8,128)(2,1)S(1)}, u32[]{:S(2)}, u32[]{:S(2)}) %collective-permute-start.42) | collective-permute-done | bytes 1048608 | tf_op jit(solution)/shard_map/ppermute | solution.py:144
  334.8 5.9 %convolution_convert_fusion = bf16[256,2048]{1,0:T(8,128)(2,1)S(1)} fusion(bf16[2048,2048]{1,0:T(8,128)(2,1)} %copy-done.2, bf16[512,2048]{1,0:T(8,128)(2,1)S(1)} %pad_maximum_fusion.3), kind=kOutput, calls=%fused_computation.11 | convolution fusion | flops 2148007936 | bytes 10485760 | tf_op jit(solution)/shard_map/dot_general | solution.py:485
  344.5 11.7 %collective-permute-done.43 = bf16[512,1024]{1,0:T(8,128)(2,1)S(1)} collective-permute-done((bf16[512,1024]{1,0:T(8,128)(2,1)}, bf16[512,1024]{1,0:T(8,128)(2,1)S(1)}, u32[]{:S(2)}, u32[]{:S(2)}) %collective-permute-start.43) | collective-permute-done | bytes 1048608 | tf_op jit(solution)/shard_map/ppermute | solution.py:144
  361.9 8.0 %collective-permute-done.34 = bf16[256,2048]{1,0:T(8,128)(2,1)S(1)} collective-permute-done((bf16[256,2048]{1,0:T(8,128)(2,1)S(1)}, bf16[256,2048]{1,0:T(8,128)(2,1)S(1)}, u32[]{:S(2)}, u32[]{:S(2)}) %collective-permute-start.34) | collective-permute-done | bytes 1048608 | tf_op jit(solution)/shard_map/ppermute | solution.py:144
  372.4 19.1 %collective-permute-done.46 = bf16[256,2048]{1,0:T(8,128)(2,1)S(1)} collective-permute-done((bf16[256,2048]{1,0:T(8,128)(2,1)S(1)}, bf16[256,2048]{1,0:T(8,128)(2,1)S(1)}, u32[]{:S(2)}, u32[]{:S(2)}) %collective-permute-start.46) | collective-permute-done | bytes 1048608 | tf_op jit(solution)/shard_map/ppermute | solution.py:144
  (305 shorter events, 186.9 us)
Async XLA Ops:
  2.5 19.0 %collective-permute-start.2 = (f32[16,128]{1,0:T(8,128)S(1)}, f32[16,128]{1,0:T(8,128)S(1)}, u32[]{:S(2)}, u32[]{:S(2)}) collective-permute-start(f32[16,128]{1,0:T(8,128)S(1)} %bitcast.29), channel_id=1, source_target_pairs={{0,4},{4,0},{8,12},{12,8},{16,20},{20,16},{24,28},{28,24},{1,5},{5... | collective-permute-start | bytes 24584 | tf_op jit(solution)/shard_map/ppermute | solution.py:144
  22.1 31.1 %collective-permute-start.3 = (bf16[512,1024]{1,0:T(8,128)(2,1)}, bf16[512,1024]{1,0:T(8,128)(2,1)}, u32[]{:S(2)}, u32[]{:S(2)}) collective-permute-start(bf16[512,1024]{1,0:T(8,128)(2,1)} %shard_map.78), channel_id=1, source_target_pairs={{0,4},{4,0},{8,12},{12,8},{16,20},{20,16},{24,28},{28,24},{1,5},{5... | collective-permute-start | bytes 3145736 | tf_op jit(solution)/shard_map/ppermute | solution.py:144
  22.2 40.0 %collective-permute-start.22 = (bf16[256,2048]{1,0:T(8,128)(2,1)}, bf16[256,2048]{1,0:T(8,128)(2,1)S(1)}, u32[]{:S(2)}, u32[]{:S(2)}) collective-permute-start(bf16[256,2048]{1,0:T(8,128)(2,1)} %get-tuple-element.33.refs_2_), channel_id=1, source_target_pairs={{0,2},{1,3},{2,0},{3,1},{4,6},{5,7},{6,4},{7,5},{8,10},{9,11},{10,... | collective-permute-start | bytes 3145736 | tf_op jit(solution)/shard_map/ppermute | solution.py:144
  24.1 45.8 %collective-permute-start.20 = (bf16[256,2048]{1,0:T(8,128)(2,1)S(1)}, bf16[256,2048]{1,0:T(8,128)(2,1)}, u32[]{:S(2)}, u32[]{:S(2)}) collective-permute-start(bf16[256,2048]{1,0:T(8,128)(2,1)S(1)} %get-tuple-element.34.refs_0_), channel_id=1, source_target_pairs={{0,2},{1,3},{2,0},{3,1},{4,6},{5,7},{6,4},{7,5},{8,10},{9,11},{10,... | collective-permute-start | bytes 3145736 | tf_op jit(solution)/shard_map/ppermute | solution.py:144
  53.2 24.9 %collective-permute-start.4 = (bf16[512,1024]{1,0:T(8,128)(2,1)}, bf16[512,1024]{1,0:T(8,128)(2,1)}, u32[]{:S(2)}, u32[]{:S(2)}) collective-permute-start(bf16[512,1024]{1,0:T(8,128)(2,1)} %shard_map.79), channel_id=1, source_target_pairs={{0,4},{4,0},{8,12},{12,8},{16,20},{20,16},{24,28},{28,24},{1,5},{5... | collective-permute-start | bytes 3145736 | tf_op jit(solution)/shard_map/ppermute | solution.py:144
  62.1 32.9 %collective-permute-start.23 = (bf16[256,2048]{1,0:T(8,128)(2,1)S(1)}, bf16[256,2048]{1,0:T(8,128)(2,1)S(1)}, u32[]{:S(2)}, u32[]{:S(2)}) collective-permute-start(bf16[256,2048]{1,0:T(8,128)(2,1)S(1)} %collective-permute-done.22.refs_2_), channel_id=1, source_target_pairs={{0,1},{1,0},{2,3},{3,2},{4,5},{5,4},{6,7},{7,6},{8,9},{9,8},{10,11... | collective-permute-start | bytes 3145736 | tf_op jit(solution)/shard_map/ppermute | solution.py:144
  70.0 25.0 %collective-permute-start.21 = (bf16[256,2048]{1,0:T(8,128)(2,1)}, bf16[256,2048]{1,0:T(8,128)(2,1)S(1)}, u32[]{:S(2)}, u32[]{:S(2)}) collective-permute-start(bf16[256,2048]{1,0:T(8,128)(2,1)} %collective-permute-done.20.refs_0_), channel_id=1, source_target_pairs={{0,1},{1,0},{2,3},{3,2},{4,5},{5,4},{6,7},{7,6},{8,9},{9,8},{10,11... | collective-permute-start | bytes 3145736 | tf_op jit(solution)/shard_map/ppermute | solution.py:144
  78.1 31.2 %collective-permute-start.12 = (bf16[512,1024]{1,0:T(8,128)(2,1)}, bf16[512,1024]{1,0:T(8,128)(2,1)}, u32[]{:S(2)}, u32[]{:S(2)}) collective-permute-start(bf16[512,1024]{1,0:T(8,128)(2,1)} %shard_map.81), channel_id=1, source_target_pairs={{0,4},{4,0},{8,12},{12,8},{16,20},{20,16},{24,28},{28,24},{1,5},{5... | collective-permute-start | bytes 3145736 | tf_op jit(solution)/shard_map/ppermute | solution.py:144
  109.3 28.3 %collective-permute-start.24 = (bf16[512,1024]{1,0:T(8,128)(2,1)}, bf16[512,1024]{1,0:T(8,128)(2,1)}, u32[]{:S(2)}, u32[]{:S(2)}) collective-permute-start(bf16[512,1024]{1,0:T(8,128)(2,1)} %shard_map.89), channel_id=1, source_target_pairs={{0,4},{4,0},{8,12},{12,8},{16,20},{20,16},{24,28},{28,24},{1,5},{5... | collective-permute-start | bytes 3145736 | tf_op jit(solution)/shard_map/ppermute | solution.py:144
  114.2 19.1 %collective-permute-start.5 = (bf16[512,512]{1,0:T(8,128)(2,1)S(1)}, bf16[512,512]{1,0:T(8,128)(2,1)S(1)}, u32[]{:S(2)}, u32[]{:S(2)}) collective-permute-start(bf16[512,512]{1,0:T(8,128)(2,1)S(1)} %get-tuple-element.29), channel_id=1, source_target_pairs={{0,8},{4,12},{8,0},{12,4},{16,24},{20,28},{24,16},{28,20},{1,9},{5... | collective-permute-start | bytes 1572872 | tf_op jit(solution)/shard_map/ppermute | solution.py:144
  124.3 30.7 %collective-permute-start.11 = (bf16[1024,256]{1,0:T(8,128)(2,1)}, bf16[1024,256]{1,0:T(8,128)(2,1)}, u32[]{:S(2)}, u32[]{:S(2)}) collective-permute-start(bf16[1024,256]{1,0:T(8,128)(2,1)} %pad_maximum_fusion.10), channel_id=1, source_target_pairs={{0,8},{4,12},{8,0},{12,4},{16,24},{20,28},{24,16},{28,20},{1,9},{5... | collective-permute-start | bytes 1572872 | tf_op jit(solution)/shard_map/ppermute | solution.py:144
  134.2 23.1 %collective-permute-start.6 = (bf16[512,256]{1,0:T(8,128)(2,1)}, bf16[512,256]{1,0:T(8,128)(2,1)}, u32[]{:S(2)}, u32[]{:S(2)}) collective-permute-start(bf16[512,256]{1,0:T(8,128)(2,1)} %fusion.26), channel_id=1, source_target_pairs={{0,16},{4,20},{8,24},{12,28},{16,0},{20,4},{24,8},{28,12},{1,17},{... | collective-permute-start | bytes 786440 | tf_op jit(solution)/shard_map/ppermute | solution.py:144
  135.1 25.7 %collective-permute-start.13 = (bf16[512,512]{1,0:T(8,128)(2,1)}, bf16[512,512]{1,0:T(8,128)(2,1)}, u32[]{:S(2)}, u32[]{:S(2)}) collective-permute-start(bf16[512,512]{1,0:T(8,128)(2,1)} %shard_map.82), channel_id=1, source_target_pairs={{0,8},{4,12},{8,0},{12,4},{16,24},{20,28},{24,16},{28,20},{1,9},{5... | collective-permute-start | bytes 1572872 | tf_op jit(solution)/shard_map/ppermute | solution.py:144
  137.6 29.5 %collective-permute-start.25 = (bf16[512,1024]{1,0:T(8,128)(2,1)}, bf16[512,1024]{1,0:T(8,128)(2,1)}, u32[]{:S(2)}, u32[]{:S(2)}) collective-permute-start(bf16[512,1024]{1,0:T(8,128)(2,1)} %shard_map.90), channel_id=1, source_target_pairs={{0,4},{4,0},{8,12},{12,8},{16,20},{20,16},{24,28},{28,24},{1,5},{5... | collective-permute-start | bytes 3145736 | tf_op jit(solution)/shard_map/ppermute | solution.py:144
  218.4 36.0 %collective-permute-start.26 = (bf16[512,1024]{1,0:T(8,128)(2,1)}, bf16[512,1024]{1,0:T(8,128)(2,1)}, u32[]{:S(2)}, u32[]{:S(2)}) collective-permute-start(bf16[512,1024]{1,0:T(8,128)(2,1)} %shard_map.91), channel_id=1, source_target_pairs={{0,4},{4,0},{8,12},{12,8},{16,20},{20,16},{24,28},{28,24},{1,5},{5... | collective-permute-start | bytes 3145736 | tf_op jit(solution)/shard_map/ppermute | solution.py:144
  219.9 19.0 %collective-permute-start.36 = (bf16[512,512]{1,0:T(8,128)(2,1)}, bf16[512,512]{1,0:T(8,128)(2,1)S(1)}, u32[]{:S(2)}, u32[]{:S(2)}) collective-permute-start(bf16[512,512]{1,0:T(8,128)(2,1)} %shard_map.101), channel_id=1, source_target_pairs={{0,8},{4,12},{8,0},{12,4},{16,24},{20,28},{24,16},{28,20},{1,9},{5... | collective-permute-start | bytes 1572872 | tf_op jit(solution)/shard_map/ppermute | solution.py:144
  228.2 24.3 %collective-permute-start.31 = (bf16[512,512]{1,0:T(8,128)(2,1)S(1)}, bf16[512,512]{1,0:T(8,128)(2,1)S(1)}, u32[]{:S(2)}, u32[]{:S(2)}) collective-permute-start(bf16[512,512]{1,0:T(8,128)(2,1)S(1)} %pad_maximum_fusion.12), channel_id=1, source_target_pairs={{0,8},{4,12},{8,0},{12,4},{16,24},{20,28},{24,16},{28,20},{1,9},{5... | collective-permute-start | bytes 1572872 | tf_op jit(solution)/shard_map/ppermute | solution.py:144
  240.9 24.2 %collective-permute-start.37 = (bf16[512,256]{1,0:T(8,128)(2,1)}, bf16[512,256]{1,0:T(8,128)(2,1)}, u32[]{:S(2)}, u32[]{:S(2)}) collective-permute-start(bf16[512,256]{1,0:T(8,128)(2,1)} %fusion.19), channel_id=1, source_target_pairs={{0,16},{4,20},{8,24},{12,28},{16,0},{20,4},{24,8},{28,12},{1,17},{... | collective-permute-start | bytes 786440 | tf_op jit(solution)/shard_map/ppermute | solution.py:144
  254.4 34.6 %collective-permute-start.32 = (bf16[512,1024]{1,0:T(8,128)(2,1)}, bf16[512,1024]{1,0:T(8,128)(2,1)}, u32[]{:S(2)}, u32[]{:S(2)}) collective-permute-start(bf16[512,1024]{1,0:T(8,128)(2,1)} %shard_map.99), channel_id=1, source_target_pairs={{0,4},{4,0},{8,12},{12,8},{16,20},{20,16},{24,28},{28,24},{1,5},{5... | collective-permute-start | bytes 3145736 | tf_op jit(solution)/shard_map/ppermute | solution.py:144
  278.1 19.8 %collective-permute-start.38 = (bf16[512,256]{1,0:T(8,128)(2,1)}, bf16[512,256]{1,0:T(8,128)(2,1)S(1)}, u32[]{:S(2)}, u32[]{:S(2)}) collective-permute-start(bf16[512,256]{1,0:T(8,128)(2,1)} %shard_map.102), channel_id=1, source_target_pairs={{0,16},{4,20},{8,24},{12,28},{16,0},{20,4},{24,8},{28,12},{1,17},{... | collective-permute-start | bytes 786440 | tf_op jit(solution)/shard_map/ppermute | solution.py:144
  306.0 25.1 %collective-permute-start.42 = (bf16[512,1024]{1,0:T(8,128)(2,1)}, bf16[512,1024]{1,0:T(8,128)(2,1)S(1)}, u32[]{:S(2)}, u32[]{:S(2)}) collective-permute-start(bf16[512,1024]{1,0:T(8,128)(2,1)} %shard_map.104), channel_id=1, source_target_pairs={{0,4},{4,0},{8,12},{12,8},{16,20},{20,16},{24,28},{28,24},{1,5},{5... | collective-permute-start | bytes 3145736 | tf_op jit(solution)/shard_map/ppermute | solution.py:144
  332.0 24.1 %collective-permute-start.43 = (bf16[512,1024]{1,0:T(8,128)(2,1)}, bf16[512,1024]{1,0:T(8,128)(2,1)S(1)}, u32[]{:S(2)}, u32[]{:S(2)}) collective-permute-start(bf16[512,1024]{1,0:T(8,128)(2,1)} %shard_map.105), channel_id=1, source_target_pairs={{0,4},{4,0},{8,12},{12,8},{16,20},{20,16},{24,28},{28,24},{1,5},{5... | collective-permute-start | bytes 3145736 | tf_op jit(solution)/shard_map/ppermute | solution.py:144
  343.9 26.0 %collective-permute-start.34 = (bf16[256,2048]{1,0:T(8,128)(2,1)S(1)}, bf16[256,2048]{1,0:T(8,128)(2,1)S(1)}, u32[]{:S(2)}, u32[]{:S(2)}) collective-permute-start(bf16[256,2048]{1,0:T(8,128)(2,1)S(1)} %copy-done.64), channel_id=1, source_target_pairs={{0,2},{1,3},{2,0},{3,1},{4,6},{5,7},{6,4},{7,5},{8,10},{9,11},{10,... | collective-permute-start | bytes 3145736 | tf_op jit(solution)/shard_map/ppermute | solution.py:144
  361.2 30.4 %collective-permute-start.46 = (bf16[256,2048]{1,0:T(8,128)(2,1)S(1)}, bf16[256,2048]{1,0:T(8,128)(2,1)S(1)}, u32[]{:S(2)}, u32[]{:S(2)}) collective-permute-start(bf16[256,2048]{1,0:T(8,128)(2,1)S(1)} %fusion.3), channel_id=1, source_target_pairs={{0,2},{1,3},{2,0},{3,1},{4,6},{5,7},{6,4},{7,5},{8,10},{9,11},{10,... | collective-permute-start | bytes 3145736 | tf_op jit(solution)/shard_map/ppermute | solution.py:144
  (93 other events, 654.1 us)
